TPU v7x, 32 devices: a whole 2x2x4 slice. The times are simulated.
32 devices in a mesh: dp: 8 (over y, x, core), fsdp: 4 (over z).
Axes of the slice: x: 2, y: 2, z: 4, core: 2. Of those that a mesh axis runs over, the one named last changes fastest.
Arguments:
- hidden: bfloat16 [20480, 768], P(('dp', 'fsdp')), may hold values from -6 to 6
- encoded: bfloat16 [65536, 768], P(('dp', 'fsdp')), may hold values from -6 to 6
- out_grad: bfloat16 [20480, 768], P(('dp', 'fsdp')), may hold values from -6 to 6
- lengths: int32 [128], P(('dp', 'fsdp')), may hold values from 64 to 256, as said below
- group_ids: int32 [128], P(('dp', 'fsdp')), may hold values from 0 to 2
- id_tags: int32 [20480], P(('dp', 'fsdp')), may hold values 0 or 1
- loss_mask: int32 [20480], P(('dp', 'fsdp')), may hold values from 0 to 1
- group_steps: int32 [3], replicated, may hold values from 0 to 9999
- group_weights: int32 [3], replicated, may hold values from 1 to 4
- gain_self: bfloat16 [768], P('fsdp'), may hold values from 0.5 to 1.5
- gain_cross: bfloat16 [768], P('fsdp'), may hold values from 0.5 to 1.5
- gain_ffn: bfloat16 [768], P('fsdp'), may hold values from 0.5 to 1.5
- rel_bias: bfloat16 [12, 32], P('fsdp'), may hold values from -4 to 4
- query_weight: bfloat16 [768, 768], P('fsdp'), may hold values from -0.109375 to 0.109375
- key_weight: bfloat16 [768, 768], P('fsdp'), may hold values from -0.109375 to 0.109375
- value_weight: bfloat16 [768, 768], P('fsdp'), may hold values from -0.21875 to 0.21875
- output_weight: bfloat16 [768, 768], P('fsdp'), may hold values from -0.625 to 0.625
- cross_query: bfloat16 [768, 768], P('fsdp'), may hold values from -0.109375 to 0.109375
- cross_key: bfloat16 [768, 768], P('fsdp'), may hold values from -0.109375 to 0.109375
- cross_value: bfloat16 [768, 768], P('fsdp'), may hold values from -0.21875 to 0.21875
- cross_output: bfloat16 [768, 768], P('fsdp'), may hold values from -0.875 to 0.875
- expand_weight: bfloat16 [768, 3072], P('fsdp'), may hold values from -0.21875 to 0.21875
- reduce_weight: bfloat16 [3072, 768], P('fsdp'), may hold values from -0.15625 to 0.15625
Outputs:
- layer_output: bfloat16 [20480, 768], P(('dp', 'fsdp'))
- grad_hidden: float32 [20480, 768], P(('dp', 'fsdp'))
- grad_encoded: float32 [65536, 768], P(('dp', 'fsdp'))
- grad_gain_self: float32 [768], P('fsdp')
- grad_gain_cross: float32 [768], P('fsdp')
- grad_gain_ffn: float32 [768], P('fsdp')
- grad_rel_bias: float32 [12, 32], P('fsdp')
- grad_query_weight: float32 [768, 768], P('fsdp')
- grad_key_weight: float32 [768, 768], P('fsdp')
- grad_value_weight: float32 [768, 768], P('fsdp')
- grad_output_weight: float32 [768, 768], P('fsdp')
- grad_cross_query: float32 [768, 768], P('fsdp')
- grad_cross_key: float32 [768, 768], P('fsdp')
- grad_cross_value: float32 [768, 768], P('fsdp')
- grad_cross_output: float32 [768, 768], P('fsdp')
- grad_expand_weight: float32 [768, 3072], P('fsdp')
- grad_reduce_weight: float32 [3072, 768], P('fsdp')
Inputs may be any that keep to these rules, and one draw needn't show every extreme that they name: `lengths`: entries b * 4 to (b + 1) * 4 - 1 are the sequences of device b of dp+fsdp and sum to 640; in each such block exactly one length is 256.
All inputs are finite; a program needn't handle non-finite values. No bound on the sum of `id_tags` on one device may be relied on, other than what follows from the above.
Results may differ from a plain program's by a relative error of at most 0.022.
The roundings to bfloat16 on the way count: a program that leaves them out, or rounds other values in their place, can miss the bound.
Values may be sent and summed in bfloat16 or wider, within the bound.
No kernel may reach another device: no remote copies, remote signals or barrier semaphores. Data moves between devices by JAX's collectives and lax.ppermute only.
A program may use at most 256 MiB of HBM per device.

v0:
```python
from functools import partial
import math

import jax
import jax.numpy as jnp
from jax import lax
from jax.sharding import PartitionSpec as P

HEADS = 12
HEAD = 64
BUCKETS = 32
MAX_DIST = 128
ENC_LEN = 512
MAX_LEN = 256
GROUPS = 3
HORIZON = 10000


epsilon = 1e-06
masked_score = -1000000000.0


def bucket_of(distance):
    exact = BUCKETS // 2
    bucket = jnp.minimum(distance, exact)
    for step in range(1, exact):
        edge = math.ceil(exact * (MAX_DIST / exact) ** (step / exact))
        bucket = bucket + (distance >= edge).astype(jnp.int32)
    return bucket


def segments_of(lengths, rows):
    positions = jnp.arange(rows, dtype=jnp.int32)
    starts = jnp.cumsum(lengths) - lengths
    segment = jnp.sum((positions[:, None] >= starts[None, :]).astype(jnp.int32), axis=1) - 1
    return (positions, starts, segment)


def token_weights(lengths, group_ids, id_tags, loss_mask, group_steps, group_weights):
    positions, starts, segment = segments_of(lengths, id_tags.shape[0])
    member = segment[:, None] == jnp.arange(lengths.shape[0], dtype=jnp.int32)[None, :]
    group_of = jnp.sum(jnp.where(member, group_ids[None, :], 0), axis=1)
    factor = (
        group_weights.astype(jnp.float32)
        * 0.25
        * (1.0 - group_steps.astype(jnp.float32) / (2.0 * HORIZON))
    )
    chosen = group_of[:, None] == jnp.arange(GROUPS, dtype=jnp.int32)[None, :]
    scale = jnp.sum(jnp.where(chosen, factor[None, :], 0.0), axis=1)
    counted = jnp.where(group_of == 1, id_tags, loss_mask).astype(jnp.float32)
    return scale * (0.25 + 0.75 * counted)


def norm_rows(rows, gain):
    scale = lax.rsqrt(jnp.mean(rows * rows, axis=-1, keepdims=True) + epsilon)
    return rows * scale * gain


def gelu_exact(inputs):
    return jax.nn.gelu(inputs, approximate=False)


def project(left, right):
    return jnp.dot(left, right, preferred_element_type=jnp.float32)


def along_rows(left, right):
    return lax.dot_general(
        left, right, (((0,), (0,)), ((), ())), preferred_element_type=jnp.float32
    )


def against(left, right):
    return lax.dot_general(
        left, right, (((1,), (1,)), ((), ())), preferred_element_type=jnp.float32
    )


def distance_bias(rel_whole, rows):
    lags = jnp.arange(rows, dtype=jnp.int32)
    table = (bucket_of(lags)[None, :] == jnp.arange(BUCKETS, dtype=jnp.int32)[:, None]).astype(
        jnp.float32
    )
    by_lag = jnp.dot(rel_whole, table, precision=lax.Precision.HIGHEST)
    heads = rel_whole.shape[0]
    period = jnp.concatenate(
        [by_lag[:, :1], jnp.zeros((heads, 1), jnp.float32), by_lag[:, :0:-1]], axis=1
    )
    return jnp.tile(period, (1, rows))[:, : rows * rows].reshape(heads, rows, rows)


def self_scores(query, keys, extra, allowed):
    raw = jnp.einsum("qhd,khd->hqk", query, keys, preferred_element_type=jnp.float32)
    return jnp.where(allowed, raw + extra, masked_score)


def softmax_parts(scores):
    top = jnp.max(scores, axis=-1, keepdims=True)
    powers = jnp.exp(scores - top)
    total = jnp.sum(powers, axis=-1, keepdims=True)
    return (powers / total, top + jnp.log(total))


def attention_back(probs, grad_mixed, query, keys, values):
    grad_probs = jnp.einsum("qhe,khe->hqk", grad_mixed, values, preferred_element_type=jnp.float32)
    grad_scores = probs * (grad_probs - jnp.sum(probs * grad_probs, axis=-1, keepdims=True))
    scores_low = grad_scores.astype(jnp.bfloat16)
    grad_query = jnp.einsum("hqk,khe->qhe", scores_low, keys, preferred_element_type=jnp.float32)
    grad_keys = jnp.einsum("hqk,qhe->khe", scores_low, query, preferred_element_type=jnp.float32)
    grad_values = jnp.einsum(
        "hqk,qhe->khe", probs.astype(jnp.bfloat16), grad_mixed, preferred_element_type=jnp.float32
    )
    return (grad_scores, grad_query, grad_keys, grad_values)


def per_device(
    hidden,
    encoded,
    out_grad,
    lengths,
    group_ids,
    id_tags,
    loss_mask,
    group_steps,
    group_weights,
    gain_self,
    gain_cross,
    gain_ffn,
    rel_bias,
    query_weight,
    key_weight,
    value_weight,
    output_weight,
    cross_query,
    cross_key,
    cross_value,
    cross_output,
    expand_weight,
    reduce_weight,
):
    rows, width = hidden.shape
    count = lengths.shape[0]
    attention_set = (
        lax.all_gather(query_weight, "fsdp", axis=0, tiled=True),
        lax.all_gather(key_weight, "fsdp", axis=0, tiled=True),
        lax.all_gather(value_weight, "fsdp", axis=0, tiled=True),
        lax.all_gather(output_weight, "fsdp", axis=0, tiled=True),
        lax.all_gather(cross_query, "fsdp", axis=0, tiled=True),
        lax.all_gather(cross_key, "fsdp", axis=0, tiled=True),
        lax.all_gather(cross_value, "fsdp", axis=0, tiled=True),
        lax.all_gather(cross_output, "fsdp", axis=0, tiled=True),
        lax.all_gather(gain_self, "fsdp", axis=0, tiled=True),
        lax.all_gather(gain_cross, "fsdp", axis=0, tiled=True),
        lax.all_gather(rel_bias, "fsdp", axis=0, tiled=True),
    )
    ffn_set = (
        lax.all_gather(expand_weight, "fsdp", axis=0, tiled=True),
        lax.all_gather(reduce_weight, "fsdp", axis=0, tiled=True),
        lax.all_gather(gain_ffn, "fsdp", axis=0, tiled=True),
    )
    (
        full_query,
        full_key,
        full_value,
        full_output,
        full_cross_query,
        full_cross_key,
        full_cross_value,
        full_cross_output,
        whole_gain_self,
        whole_gain_cross,
        whole_rel,
    ) = attention_set
    full_expand, full_reduce, whole_gain_ffn = ffn_set
    gain_one = whole_gain_self.astype(jnp.float32)
    gain_two = whole_gain_cross.astype(jnp.float32)
    gain_three = whole_gain_ffn.astype(jnp.float32)
    positions, starts, segment = segments_of(lengths, rows)
    lag = positions[:, None] - positions[None, :]
    allowed = ((segment[:, None] == segment[None, :]) & (lag >= 0))[None]
    extra, bias_pull = jax.vjp(partial(distance_bias, rows=rows), whole_rel.astype(jnp.float32))
    hidden_wide = hidden.astype(jnp.float32)
    normed_one = norm_rows(hidden_wide, gain_one).astype(jnp.bfloat16)
    query = project(normed_one, full_query).astype(jnp.bfloat16).reshape(rows, HEADS, HEAD)
    keys = project(normed_one, full_key).astype(jnp.bfloat16).reshape(rows, HEADS, HEAD)
    values = project(normed_one, full_value).astype(jnp.bfloat16).reshape(rows, HEADS, HEAD)
    probs, self_lse = softmax_parts(self_scores(query, keys, extra, allowed))
    mixed = jnp.einsum(
        "hqk,khe->qhe", probs.astype(jnp.bfloat16), values, preferred_element_type=jnp.float32
    )
    mixed = mixed.reshape(rows, width).astype(jnp.bfloat16)
    hidden_one = hidden_wide + project(mixed, full_output)
    normed_two = norm_rows(hidden_one, gain_two).astype(jnp.bfloat16)
    cross_q = project(normed_two, full_cross_query).astype(jnp.bfloat16)
    cross_k = (
        project(encoded, full_cross_key).astype(jnp.bfloat16).reshape(count, ENC_LEN, HEADS, HEAD)
    )
    cross_v = (
        project(encoded, full_cross_value).astype(jnp.bfloat16).reshape(count, ENC_LEN, HEADS, HEAD)
    )
    padded_q = jnp.concatenate([cross_q, jnp.zeros((MAX_LEN, width), jnp.bfloat16)], axis=0)
    window = jnp.arange(MAX_LEN, dtype=jnp.int32)
    cross_sum = jnp.zeros((rows + MAX_LEN, width), jnp.float32)
    cross_lse = []
    for index in range(count):
        valid = (window < lengths[index])[:, None]
        piece_q = lax.dynamic_slice_in_dim(padded_q, starts[index], MAX_LEN, 0).reshape(
            MAX_LEN, HEADS, HEAD
        )
        piece_scores = jnp.einsum(
            "qhd,khd->hqk", piece_q, cross_k[index], preferred_element_type=jnp.float32
        )
        piece_probs, piece_lse = softmax_parts(piece_scores)
        piece_out = jnp.einsum(
            "hqk,khe->qhe",
            piece_probs.astype(jnp.bfloat16),
            cross_v[index],
            preferred_element_type=jnp.float32,
        ).reshape(MAX_LEN, width)
        current = lax.dynamic_slice_in_dim(cross_sum, starts[index], MAX_LEN, 0)
        cross_sum = lax.dynamic_update_slice_in_dim(
            cross_sum, current + jnp.where(valid, piece_out, 0.0), starts[index], 0
        )
        cross_lse.append(piece_lse)
    crossed = cross_sum[:rows].astype(jnp.bfloat16)
    hidden_two = hidden_one + project(crossed, full_cross_output)
    normed_three = norm_rows(hidden_two, gain_three).astype(jnp.bfloat16)
    expanded = project(normed_three, full_expand)
    activated, gelu_pull = jax.vjp(gelu_exact, expanded)
    activated_low = activated.astype(jnp.bfloat16)
    layer_output = (hidden_two + project(activated_low, full_reduce)).astype(jnp.bfloat16)
    scaled = (
        out_grad.astype(jnp.float32)
        * token_weights(lengths, group_ids, id_tags, loss_mask, group_steps, group_weights)[:, None]
    )
    scaled_low = scaled.astype(jnp.bfloat16)
    back_expand, back_reduce = (
        lax.all_gather(expand_weight, "fsdp", axis=0, tiled=True),
        lax.all_gather(reduce_weight, "fsdp", axis=0, tiled=True),
    )
    grad_activated = against(scaled_low, back_reduce)
    (grad_expanded,) = gelu_pull(grad_activated)
    grad_expanded_low = grad_expanded.astype(jnp.bfloat16)
    ffn_shards = (
        lax.psum_scatter(
            along_rows(normed_three, grad_expanded_low), "fsdp", scatter_dimension=0, tiled=True
        ),
        lax.psum_scatter(
            along_rows(activated_low, scaled_low), "fsdp", scatter_dimension=0, tiled=True
        ),
    )
    grad_expand_shard, grad_reduce_shard = ffn_shards
    _, norm_pull = jax.vjp(norm_rows, hidden_two, gain_three)
    grad_norm_part, grad_gain_three = norm_pull(against(grad_expanded_low, back_expand))
    grad_two = scaled + grad_norm_part
    (
        back_query,
        back_key,
        back_value,
        back_output,
        back_cross_query,
        back_cross_key,
        back_cross_value,
        back_cross_output,
    ) = (
        lax.all_gather(query_weight, "fsdp", axis=0, tiled=True),
        lax.all_gather(key_weight, "fsdp", axis=0, tiled=True),
        lax.all_gather(value_weight, "fsdp", axis=0, tiled=True),
        lax.all_gather(output_weight, "fsdp", axis=0, tiled=True),
        lax.all_gather(cross_query, "fsdp", axis=0, tiled=True),
        lax.all_gather(cross_key, "fsdp", axis=0, tiled=True),
        lax.all_gather(cross_value, "fsdp", axis=0, tiled=True),
        lax.all_gather(cross_output, "fsdp", axis=0, tiled=True),
    )
    branch_two = grad_two.astype(jnp.bfloat16)
    grad_cross_output = along_rows(crossed, branch_two)
    grad_crossed = against(branch_two, back_cross_output).astype(jnp.bfloat16)
    padded_grad = jnp.concatenate([grad_crossed, jnp.zeros((MAX_LEN, width), jnp.bfloat16)], axis=0)
    query_sum = jnp.zeros((rows + MAX_LEN, width), jnp.float32)
    key_parts = []
    value_parts = []
    for index in range(count):
        valid = (window < lengths[index])[:, None]
        piece_q = lax.dynamic_slice_in_dim(padded_q, starts[index], MAX_LEN, 0).reshape(
            MAX_LEN, HEADS, HEAD
        )
        piece_grad = jnp.where(
            valid, lax.dynamic_slice_in_dim(padded_grad, starts[index], MAX_LEN, 0), 0
        ).reshape(MAX_LEN, HEADS, HEAD)
        piece_scores = jnp.einsum(
            "qhd,khd->hqk", piece_q, cross_k[index], preferred_element_type=jnp.float32
        )
        piece_probs = jnp.exp(piece_scores - cross_lse[index])
        _, grad_query_piece, grad_key_piece, grad_value_piece = attention_back(
            piece_probs, piece_grad, piece_q, cross_k[index], cross_v[index]
        )
        current = lax.dynamic_slice_in_dim(query_sum, starts[index], MAX_LEN, 0)
        query_sum = lax.dynamic_update_slice_in_dim(
            query_sum, current + grad_query_piece.reshape(MAX_LEN, width), starts[index], 0
        )
        key_parts.append(grad_key_piece.reshape(ENC_LEN, width))
        value_parts.append(grad_value_piece.reshape(ENC_LEN, width))
    grad_cq_low = query_sum[:rows].astype(jnp.bfloat16)
    grad_ck_low = jnp.concatenate(key_parts, axis=0).astype(jnp.bfloat16)
    grad_cv_low = jnp.concatenate(value_parts, axis=0).astype(jnp.bfloat16)
    grad_cross_query = along_rows(normed_two, grad_cq_low)
    grad_cross_key = along_rows(encoded, grad_ck_low)
    grad_cross_value = along_rows(encoded, grad_cv_low)
    grad_encoded = against(grad_ck_low, back_cross_key) + against(grad_cv_low, back_cross_value)
    _, norm_pull = jax.vjp(norm_rows, hidden_one, gain_two)
    grad_norm_part, grad_gain_two = norm_pull(against(grad_cq_low, back_cross_query))
    grad_one = grad_two + grad_norm_part
    branch_one = grad_one.astype(jnp.bfloat16)
    grad_output = along_rows(mixed, branch_one)
    grad_mixed = against(branch_one, back_output).astype(jnp.bfloat16).reshape(rows, HEADS, HEAD)
    probs = jnp.exp(self_scores(query, keys, extra, allowed) - self_lse)
    grad_scores, grad_q, grad_k, grad_v = attention_back(probs, grad_mixed, query, keys, values)
    (grad_rel,) = bias_pull(grad_scores)
    grad_q_low = grad_q.reshape(rows, width).astype(jnp.bfloat16)
    grad_k_low = grad_k.reshape(rows, width).astype(jnp.bfloat16)
    grad_v_low = grad_v.reshape(rows, width).astype(jnp.bfloat16)
    grad_query = along_rows(normed_one, grad_q_low)
    grad_key = along_rows(normed_one, grad_k_low)
    grad_value = along_rows(normed_one, grad_v_low)
    grad_normed_one = (
        against(grad_q_low, back_query)
        + against(grad_k_low, back_key)
        + against(grad_v_low, back_value)
    )
    _, norm_pull = jax.vjp(norm_rows, hidden_wide, gain_one)
    grad_norm_part, grad_gain_one = norm_pull(grad_normed_one)
    grad_hidden = grad_one + grad_norm_part
    (
        shard_query,
        shard_key,
        shard_value,
        shard_output,
        shard_cross_query,
        shard_cross_key,
        shard_cross_value,
        shard_cross_output,
        shard_gain_one,
        shard_gain_two,
        shard_gain_three,
        shard_rel,
    ) = (
        lax.psum_scatter(grad_query, "fsdp", scatter_dimension=0, tiled=True),
        lax.psum_scatter(grad_key, "fsdp", scatter_dimension=0, tiled=True),
        lax.psum_scatter(grad_value, "fsdp", scatter_dimension=0, tiled=True),
        lax.psum_scatter(grad_output, "fsdp", scatter_dimension=0, tiled=True),
        lax.psum_scatter(grad_cross_query, "fsdp", scatter_dimension=0, tiled=True),
        lax.psum_scatter(grad_cross_key, "fsdp", scatter_dimension=0, tiled=True),
        lax.psum_scatter(grad_cross_value, "fsdp", scatter_dimension=0, tiled=True),
        lax.psum_scatter(grad_cross_output, "fsdp", scatter_dimension=0, tiled=True),
        lax.psum_scatter(grad_gain_one, "fsdp", scatter_dimension=0, tiled=True),
        lax.psum_scatter(grad_gain_two, "fsdp", scatter_dimension=0, tiled=True),
        lax.psum_scatter(grad_gain_three, "fsdp", scatter_dimension=0, tiled=True),
        lax.psum_scatter(grad_rel, "fsdp", scatter_dimension=0, tiled=True),
    )
    totals = lax.psum(
        (
            shard_query,
            shard_key,
            shard_value,
            shard_output,
            shard_cross_query,
            shard_cross_key,
            shard_cross_value,
            shard_cross_output,
            shard_gain_one,
            shard_gain_two,
            shard_gain_three,
            shard_rel,
            grad_expand_shard,
            grad_reduce_shard,
        ),
        "dp",
    )
    return (
        layer_output,
        grad_hidden,
        grad_encoded,
        totals[8],
        totals[9],
        totals[10],
        totals[11],
        totals[0],
        totals[1],
        totals[2],
        totals[3],
        totals[4],
        totals[5],
        totals[6],
        totals[7],
        totals[12],
        totals[13],
    )


def solution(mesh):
    return jax.shard_map(
        per_device,
        mesh=mesh,
        in_specs=(
            P(("dp", "fsdp"), None),
            P(("dp", "fsdp"), None),
            P(("dp", "fsdp"), None),
            P(("dp", "fsdp")),
            P(("dp", "fsdp")),
            P(("dp", "fsdp")),
            P(("dp", "fsdp")),
            P(),
            P(),
            P("fsdp"),
            P("fsdp"),
            P("fsdp"),
            P("fsdp", None),
            P("fsdp", None),
            P("fsdp", None),
            P("fsdp", None),
            P("fsdp", None),
            P("fsdp", None),
            P("fsdp", None),
            P("fsdp", None),
            P("fsdp", None),
            P("fsdp", None),
            P("fsdp", None),
        ),
        out_specs=(
            P(("dp", "fsdp"), None),
            P(("dp", "fsdp"), None),
            P(("dp", "fsdp"), None),
            P("fsdp"),
            P("fsdp"),
            P("fsdp"),
            P("fsdp", None),
            P("fsdp", None),
            P("fsdp", None),
            P("fsdp", None),
            P("fsdp", None),
            P("fsdp", None),
            P("fsdp", None),
            P("fsdp", None),
            P("fsdp", None),
            P("fsdp", None),
            P("fsdp", None),
        ),
        check_vma=False,
    )
```

profile of v0, /device:TPU:9, one launch (start us, length us, event | category | flops | bytes accessed | tf_op | source)
XLA Modules:
  0.0 1443.4 jit_solution(6041928000662146957)
XLA Ops:
  29.2 11.1 all-reduce.14
  43.6 9.9 tile.4
  53.5 34.0 %tile.10 = f32[12,410240]{1,0:T(8,128)} reshape(f32[12,640,641]{2,1,0:T(8,128)} %tile.4) | data formatting | bytes 39383040 | tf_op jit(solution)/shard_map/jvp()/tile | solution.py:89
  96.1 10.1 copy.162
  106.1 15.1 %slice.150 = f32[12,640,640]{2,1,0:T(8,128)} slice(f32[16,640,640]{2,1,0:T(8,128)} %bitcast.205), slice={[0:12], [0:640], [0:640]} | slice | bytes 39321600 | tf_op jit(solution)/shard_map/jvp()/reshape | solution.py:89
  121.3 21.9 %copy.129 = f32[12,640,640]{1,2,0:T(8,128)} copy(f32[12,640,640]{2,1,0:T(8,128)} %slice.150) | data formatting | bytes 39321600 | tf_op jit(solution)/shard_map/jvp()/reshape | solution.py:89
  173.7 17.9 %fusion.140 = (f32[12,640]{1,0:T(8,128)}, f32[12,640,640]{1,2,0:T(8,128)}) fusion(f32[12,640,640]{1,2,0:T(8,128)} %copy.129, bf16[640,12,64]{0,2,1:T(8,128)(2,1)} %bitcast.210, bf16[640,12,64]{0,2,1:T(8,128)(2,1)} %bitcast.208, pred[640,640]{0,1:T(8,128)(4,1)S(1)} %fusion.50), kind=kOutput, calls=%fused_computation.247 | convolution fusion | flops 643883520 | bytes 41728000 | tf_op jit(solution)/shard_map/qhd,khd->hqk/dot_general | solution.py:93
  191.5 9.2 fusion
  200.8 11.8 fusion.57
  310.6 36.4 %all-gather.28.cloned.1.call-done = bf16[768,3072]{1,0:T(8,128)(2,1)} async-done(((bf16[192,3072]{1,0:T(8,128)(2,1)}), bf16[768,3072]{1,0:T(8,128)(2,1)}) %all-gather.28.cloned.1.call-update) | async-done | bytes 4718608 | tf_op jit(solution)/shard_map/all_gather | solution.py:157
  347.0 23.5 %multiply_convert_fusion = (bf16[640,3072]{1,0:T(8,128)(2,1)}, f32[640,3072]{1,0:T(8,128)}, f32[640,3072]{1,0:T(8,128)}) fusion(bf16[768,3072]{1,0:T(8,128)(2,1)} %all-gather.28.cloned.1.call-done, f32[640,768]{1,0:T(8,128)} %get-tuple-element.153, f32[768]{0:T(1024)S(1)} %copy-done.72, f32[640]{0:T(1024)S(1)} %fusion.117), kind=kOutput, calls=%fused_computation.14 | convolution fusion | flops 3149168640 | bytes 26351104 | tf_op jit(solution)/shard_map/dot_general | solution.py:64
  370.5 65.9 %all-gather.30.cloned.1.call-done = bf16[3072,768]{1,0:T(8,128)(2,1)} async-done(((bf16[768,768]{1,0:T(8,128)(2,1)}), bf16[3072,768]{1,0:T(8,128)(2,1)}) %all-gather.30.cloned.1.call-update) | async-done | bytes 4718608 | tf_op jit(solution)/shard_map/all_gather | solution.py:158
  436.4 11.7 add_convert_fusion
  609.7 17.7 %multiply_reduce_fusion = (f32[12,640]{1,0:T(8,128)S(1)}, f32[12,640,640]{1,2,0:T(8,128)}) fusion(f32[12,640,640]{1,2,0:T(8,128)} %get-tuple-element.141, f32[12,640]{1,0:T(8,128)S(1)} %log_add_fusion, bf16[640,12,64]{0,2,1:T(8,128)(2,1)} %bitcast.206, bf16[640,12,64]{0,2,1:T(8,128)(2,1)} %bitcast.221), kind=kOutput, calls=%fused_computation.1 | convolution fusion | flops 643883520 | bytes 41349120 | tf_op jit(solution)/shard_map/qhe,khe->hqk/dot_general | solution.py:105
  627.4 21.3 %subtract_multiply_fusion = f32[12,640,640]{1,2,0:T(8,128)} fusion(f32[12,640,640]{1,2,0:T(8,128)} %get-tuple-element.166, f32[12,640,640]{1,2,0:T(8,128)} %get-tuple-element.141, f32[12,640]{1,0:T(8,128)S(1)} %get-tuple-element.165, f32[12,640]{1,0:T(8,128)S(1)} %log_add_fusion), kind=kLoop, calls=%fused_computation | loop fusion | flops 14745600 | bytes 59043840 | tf_op jit(solution)/shard_map/mul | solution.py:106
  648.7 9.9 fusion.54
  675.1 10.4 fusion.58
  689.3 10.3 fusion.123
  699.7 9.9 fusion.80
  714.6 33.7 %reduce-scatter.25.cloned.1.call-done = f32[192,768]{1,0:T(8,128)} async-done(((f32[768,768]{1,0:T(8,128)}), f32[192,768]{1,0:T(8,128)}) %reduce-scatter.25.cloned.1.call-update) | async-done | bytes 589840 | tf_op jit(solution)/shard_map/reduce_scatter | solution.py:354
  748.2 50.3 %reduce-scatter.17.cloned.1.call-done = f32[192,768]{1,0:T(8,128)} async-done(((f32[768,768]{1,0:T(8,128)}), f32[192,768]{1,0:T(8,128)}) %reduce-scatter.17.cloned.1.call-update) | async-done | bytes 589840 | tf_op jit(solution)/shard_map/reduce_scatter | solution.py:348
  798.5 50.3 %reduce-scatter.15.cloned.1.call-done = f32[192,768]{1,0:T(8,128)} async-done(((f32[768,768]{1,0:T(8,128)}), f32[192,768]{1,0:T(8,128)}) %reduce-scatter.15.cloned.1.call-update) | async-done | bytes 589840 | tf_op jit(solution)/shard_map/reduce_scatter | solution.py:347
  848.8 50.3 %reduce-scatter.19.cloned.1.call-done = f32[192,768]{1,0:T(8,128)} async-done(((f32[768,768]{1,0:T(8,128)}), f32[192,768]{1,0:T(8,128)}) %reduce-scatter.19.cloned.1.call-update) | async-done | bytes 589840 | tf_op jit(solution)/shard_map/reduce_scatter | solution.py:349
  899.1 165.4 %reduce-scatter.27.cloned.1.call-done = f32[192,3072]{1,0:T(8,128)} async-done(((f32[768,3072]{1,0:T(8,128)}), f32[192,3072]{1,0:T(8,128)}) %reduce-scatter.27.cloned.1.call-update) | async-done | bytes 2359312 | tf_op jit(solution)/shard_map/reduce_scatter | solution.py:245
  1064.5 164.4 %reduce-scatter.29.cloned.1.call-done = f32[768,768]{1,0:T(8,128)} async-done(((f32[3072,768]{1,0:T(8,128)}), f32[768,768]{1,0:T(8,128)}) %reduce-scatter.29.cloned.1.call-update) | async-done | bytes 2359312 | tf_op jit(solution)/shard_map/reduce_scatter | solution.py:248
  1230.2 21.3 %copy.151 = f32[12,640,640]{2,1,0:T(8,128)} copy(f32[12,640,640]{1,2,0:T(8,128)} %subtract_multiply_fusion) | data formatting | bytes 39321600 | tf_op jit(solution)/shard_map/mul | solution.py:106
  1259.7 33.4 %copy.163 = f32[2,8,640,640]{3,1,2,0:T(8,128)} copy(f32[2,8,640,640]{3,2,1,0:T(8,128)S(1)} %bitcast.203) | data formatting | bytes 52428800
  1293.1 17.5 %pad.11 = f32[12,410240]{1,0:T(8,128)} pad(f32[12,409600]{1,0:T(8,128)} %bitcast.204, f32[]{:T(128)} %constant.61.clone.1), padding=0_0x0_640 | pad | bytes 39352324 | tf_op jit(solution)/shard_map/transpose(jvp())/pad | solution.py:89
  1310.6 45.5 %reshape.475 = f32[12,640,641]{2,1,0:T(8,128)} reshape(f32[12,410240]{1,0:T(8,128)} %pad.11) | data formatting | bytes 39383040 | tf_op jit(solution)/shard_map/transpose(jvp())/reshape | solution.py:89
  1356.1 9.7 reduce_sum.269
  1374.0 13.0 all-reduce.13
  1387.2 15.7 %all-reduce.11 = (f32[192]{0:T(256)}, f32[192]{0:T(256)}, f32[192]{0:T(256)}, f32[3,32]{1,0:T(4,128)}) all-reduce(f32[192]{0:T(256)S(1)} %dynamic-slice.4, f32[192]{0:T(256)S(1)} %dynamic-slice.6, f32[192]{0:T(256)S(1)} %dynamic-slice.8, f32[3,32]{1,0:T(4,128)S(1)} %constant_dynamic-slice_fusion), channel_id=1, replica_groups=mesh['dp'=8,'fsdp'=4] {'dp'}, use_global_device_ids=true, to_apply=%region_27.28 | all-reduce | flops 672 | bytes 5376 | tf_op jit(solution)/shard_map/psum | solution.py:360
  (514 shorter events, 389.0 us)
Async XLA Ops:
  7.2 216.4 %copy-start = (bf16[2048,768]{1,0:T(8,128)(2,1)S(1)}, bf16[2048,768]{1,0:T(8,128)(2,1)}, u32[]{:S(2)}) copy-start(bf16[2048,768]{1,0:T(8,128)(2,1)} %param.24) | copy-start | bytes 9437188
  7.2 20.0 %copy-start.122 = (u32[32]{0:T(128)S(1)}, u32[32]{0:T(128)}, u32[]{:S(2)}) copy-start(u32[32]{0:T(128)} %constant.153) | copy-start | bytes 388
  7.2 21.3 %copy-start.129 = (bf16[192]{0:T(256)(128)(2,1)S(1)}, bf16[192]{0:T(256)(128)(2,1)}, u32[]{:S(2)}) copy-start(bf16[192]{0:T(256)(128)(2,1)} %param.32) | copy-start | bytes 1156
  7.2 21.5 %copy-start.130 = (bf16[192]{0:T(256)(128)(2,1)S(1)}, bf16[192]{0:T(256)(128)(2,1)}, u32[]{:S(2)}) copy-start(bf16[192]{0:T(256)(128)(2,1)} %param.33) | copy-start | bytes 1156
  7.3 21.7 %copy-start.131 = (bf16[192]{0:T(256)(128)(2,1)S(1)}, bf16[192]{0:T(256)(128)(2,1)}, u32[]{:S(2)}) copy-start(bf16[192]{0:T(256)(128)(2,1)} %param.34) | copy-start | bytes 1156
  7.3 149.1 %all-gather.14.cloned.1.call-start = ((), (), s32[]{:S(2)}) async-start(), calls=%async_computation.11 | async-start | bytes 1474560 | tf_op jit(solution)/shard_map/all_gather | solution.py:144
  8.0 154.1 %all-gather.16.cloned.1.call-start = ((), (), s32[]{:S(2)}) async-start(), calls=%async_computation.12 | async-start | bytes 1474560 | tf_op jit(solution)/shard_map/all_gather | solution.py:145
  8.8 159.2 %all-gather.12.cloned.1.call-start = ((), (), s32[]{:S(2)}) async-start(), calls=%async_computation.10 | async-start | bytes 1474560 | tf_op jit(solution)/shard_map/all_gather | solution.py:146
  9.5 203.1 %all-gather.18.cloned.1.call-start = ((), (), s32[]{:S(2)}) async-start(), calls=%async_computation.13 | async-start | bytes 1474560 | tf_op jit(solution)/shard_map/all_gather | solution.py:147
  10.1 207.3 %all-gather.22.cloned.1.call-start = ((), (), s32[]{:S(2)}) async-start(), calls=%async_computation.15 | async-start | bytes 1474560 | tf_op jit(solution)/shard_map/all_gather | solution.py:148
  10.7 213.0 %all-gather.24.cloned.1.call-start = ((), (), s32[]{:S(2)}) async-start(), calls=%async_computation.16 | async-start | bytes 1474560 | tf_op jit(solution)/shard_map/all_gather | solution.py:149
  11.2 218.5 %all-gather.20.cloned.1.call-start = ((), (), s32[]{:S(2)}) async-start(), calls=%async_computation.14 | async-start | bytes 1474560 | tf_op jit(solution)/shard_map/all_gather | solution.py:150
  12.0 291.2 %all-gather.26.cloned.1.call-start = ((), (), s32[]{:S(2)}) async-start(), calls=%async_computation.17 | async-start | bytes 1474560 | tf_op jit(solution)/shard_map/all_gather | solution.py:151
  12.7 334.3 %all-gather.28.cloned.1.call-start = ((), (), s32[]{:S(2)}) async-start(), calls=%async_computation.18 | async-start | bytes 5898240 | tf_op jit(solution)/shard_map/all_gather | solution.py:157
  13.5 422.9 %all-gather.30.cloned.1.call-start = ((), (), s32[]{:S(2)}) async-start(), calls=%async_computation.19 | async-start | bytes 5898240 | tf_op jit(solution)/shard_map/all_gather | solution.py:158
  14.0 696.0 %reduce-scatter.33.cloned.1.call-start = ((), (), s32[]{:S(2)}) async-start(), calls=%async_computation.29 | async-start | bytes 2949120
  303.2 43.8 %copy-start.72 = (f32[768]{0:T(1024)S(1)}, f32[768]{0:T(1024)}, u32[]{:S(2)}) copy-start(f32[768]{0:T(1024)} %convert_element_type.341) | copy-start | bytes 9220
  347.0 89.4 %copy-start.111 = (f32[640]{0:T(1024)S(1)}, f32[640]{0:T(1024)}, u32[]{:S(2)}) copy-start(f32[640]{0:T(1024)} %add_multiply_fusion) | copy-start | bytes 7684
  502.3 210.0 %reduce-scatter.31.cloned.1.call-start = ((), (), s32[]{:S(2)}) async-start(), calls=%async_computation.28 | async-start | bytes 2949120
  502.4 13.6 slice-start.2
  510.3 19.1 %copy-start.59 = (bf16[12,64,512]{2,1,0:T(8,128)(2,1)}, bf16[12,64,512]{2,1,0:T(8,128)(2,1)S(1)}, u32[]{:S(2)}) copy-start(bf16[12,64,512]{2,1,0:T(8,128)(2,1)S(1)} %convolution_convert_fusion.11) | copy-start | bytes 2359300
  537.4 177.1 %reduce-scatter.23.cloned.1.call-start = ((), (), s32[]{:S(2)}) async-start(), calls=%async_computation.24 | async-start | bytes 2949120 | tf_op jit(solution)/shard_map/reduce_scatter | solution.py:351
  589.6 124.9 %reduce-scatter.21.cloned.1.call-start = ((), (), s32[]{:S(2)}) async-start(), calls=%async_computation.23 | async-start | bytes 2949120 | tf_op jit(solution)/shard_map/reduce_scatter | solution.py:350
  598.4 149.8 %reduce-scatter.25.cloned.1.call-start = ((), (), s32[]{:S(2)}) async-start(), calls=%async_computation.25 | async-start | bytes 2949120 | tf_op jit(solution)/shard_map/reduce_scatter | solution.py:354
  603.2 195.3 %reduce-scatter.17.cloned.1.call-start = ((), (), s32[]{:S(2)}) async-start(), calls=%async_computation.21 | async-start | bytes 2949120 | tf_op jit(solution)/shard_map/reduce_scatter | solution.py:348
  627.4 21.3 %copy-start.19 = (bf16[640,768]{0,1:T(8,128)(2,1)S(1)}, bf16[640,768]{0,1:T(8,128)(2,1)}, u32[]{:S(2)}) copy-start(bf16[640,768]{0,1:T(8,128)(2,1)} %copy.127) | copy-start | bytes 2949124
  662.3 186.5 %reduce-scatter.15.cloned.1.call-start = ((), (), s32[]{:S(2)}) async-start(), calls=%async_computation.20 | async-start | bytes 2949120 | tf_op jit(solution)/shard_map/reduce_scatter | solution.py:347
  674.9 224.2 %reduce-scatter.19.cloned.1.call-start = ((), (), s32[]{:S(2)}) async-start(), calls=%async_computation.22 | async-start | bytes 2949120 | tf_op jit(solution)/shard_map/reduce_scatter | solution.py:349
  689.2 375.3 %reduce-scatter.27.cloned.1.call-start = ((), (), s32[]{:S(2)}) async-start(), calls=%async_computation.26 | async-start | bytes 11796480 | tf_op jit(solution)/shard_map/reduce_scatter | solution.py:245
  699.6 529.2 %reduce-scatter.29.cloned.1.call-start = ((), (), s32[]{:S(2)}) async-start(), calls=%async_computation.27 | async-start | bytes 11796480 | tf_op jit(solution)/shard_map/reduce_scatter | solution.py:248
  709.6 710.8 %all-reduce.17.cloned.1.call-start = ((), (), s32[]{:S(2)}) async-start(), calls=%async_computation.30 | async-start | bytes 19660800 | tf_op jit(solution)/shard_map/psum | solution.py:360
  1371.3 31.7 %copy-start.105 = (f32[640]{0:T(1024)S(1)}, f32[640]{0:T(1024)}, u32[]{:S(2)}) copy-start(f32[640]{0:T(1024)} %copy-done.104) | copy-start | bytes 7684
  (131 other events, 610.7 us)
Sparse Core Ops, SparseCore 0:
  9.7 31.3 all-gather.13
  42.6 29.5 all-gather.15
  73.8 29.5 all-gather.11
  104.8 29.5 all-gather.17
  135.8 29.5 all-gather.21
  166.8 29.5 all-gather.23
  198.0 29.5 all-gather.19
  229.2 29.5 all-gather.25
  260.3 86.6 all-gather.27
  348.4 87.9 all-gather.29
  502.5 46.7 reduce-scatter.32
  551.4 47.5 reduce-scatter.30
  601.2 47.5 reduce-scatter.22
  651.0 47.5 reduce-scatter.20
  700.7 47.5 reduce-scatter.24
  751.0 47.5 reduce-scatter.16
  801.3 47.5 reduce-scatter.14
  851.6 47.5 reduce-scatter.18
  901.5 162.9 reduce-scatter.26
  1066.7 162.1 reduce-scatter.28
  1234.4 146.7 all-reduce.16
where the time goes:
time: 1460 us; the launch traced here: 1440 us
  waiting for transfers between devices  623 us (43%)
  local copies, waits for them, and re-layouts  351 us (24%)
  matrix products  297 us (20%)
  other arithmetic  98.2 us (7%)
  blocking collectives  46 us (3%)
  between operations  26.1 us (2%)
    reduce_scatter x1, waiting for transfers between devices, per_device(): lax.psum_scatter(along_rows(normed_three, grad_expanded_low), 'fsdp', sca...  165 us
    reduce_scatter x1, waiting for transfers between devices, per_device(): lax.psum_scatter(along_rows(activated_low, scaled_low), 'fsdp', scatter_d...  164 us
    unnamed x315, local copies, waits for them, and re-layouts  101 us
    reshape x3, local copies, waits for them, and re-layouts, distance_bias(): jnp.tile(period, (1, rows))[:, :rows * rows].reshape(heads, rows, rows)  82.5 us
    all_gather x1, waiting for transfers between devices, per_device(): lax.all_gather(reduce_weight, 'fsdp', axis=0, tiled=True)  65.9 us
    dot_general x10, matrix products, project(): return jnp.dot(left, right, preferred_element_type=jnp.float32)  58.4 us
    reduce_scatter x1, waiting for transfers between devices, per_device(): lax.psum_scatter(grad_key, 'fsdp', scatter_dimension=0, tiled=True)  50.3 us
    reduce_scatter x1, waiting for transfers between devices, per_device(): lax.psum_scatter(grad_value, 'fsdp', scatter_dimension=0, tiled=True)  50.3 us
  transfers between devices with their start and end apart: 21, of which 8 were waited for; matrix products, arithmetic and copies ran while one was open for 44% of the time, Pallas kernels for 0%

commit v1 on v0

v1 whole, which is shorter than its diff:
```python
from functools import partial
import math

import jax
import jax.numpy as jnp
import numpy as np
from jax import lax
from jax.experimental import pallas as pl
from jax.experimental.pallas import tpu as pltpu
from jax.sharding import PartitionSpec as P

HEADS = 12
HEAD = 64
PAIRS = 6
BUCKETS = 32
MAX_DIST = 128
ENC_LEN = 512
MAX_LEN = 256
GROUPS = 3
HORIZON = 10000
D = 768
COLS = 256

f32 = jnp.float32
bf16 = jnp.bfloat16
epsilon = 1e-06
masked_score = -1000000000.0

VMEM = pl.BlockSpec(memory_space=pltpu.VMEM)
SMEM = pl.BlockSpec(memory_space=pltpu.SMEM)
LIMIT = 60 * 1024 * 1024


def dot(left, right):
    return jnp.dot(left, right, preferred_element_type=f32)


def dot_nt(left, right):
    return lax.dot_general(left, right, (((1,), (1,)), ((), ())), preferred_element_type=f32)


def dot_tn(left, right):
    return lax.dot_general(left, right, (((0,), (0,)), ((), ())), preferred_element_type=f32)


def rounded(value):
    return value.astype(bf16).astype(f32)


def row_scale(rows):
    return lax.rsqrt(jnp.mean(rows * rows, axis=-1, keepdims=True) + epsilon)


def row_blocks(rows):
    return [slice(r, r + 128) for r in range(0, rows, 128)]


def col_blocks(width=D):
    return [slice(c, c + COLS) for c in range(0, width, COLS)]


def starts_of(len_ref):
    starts = [0]
    for s in range(3):
        starts.append(starts[-1] + len_ref[s])
    return starts


def norm_back(grad, rows, gain):
    r = row_scale(rows)
    pulled = gain * grad
    inner = jnp.mean(pulled * rows, axis=-1, keepdims=True)
    return r * pulled - rows * (r * r * r * inner), grad * rows * r


def split_three(value):
    high = value.astype(bf16)
    rest = value - high.astype(f32)
    mid = rest.astype(bf16)
    return high, mid, (rest - mid.astype(f32)).astype(bf16)


def weight_of(ref, index):
    return ref[:, index].reshape(D, D)


def weight_cols(ref, index, cols):
    return ref[:, index, :, cols].reshape(D, COLS)


def put_pairs(dst, cb, value):
    first = cb.start // 128
    dst[first, 0:value.shape[0], :] = value[:, :128]
    dst[first + 1, 0:value.shape[0], :] = value[:, 128:]


def clear_tail(dst, rows):
    dst[:, rows:, :] = jnp.zeros((PAIRS, dst.shape[1] - rows, 128), f32)


def join_pairs(dst, src, rows):
    for hp in range(PAIRS):
        dst[:, hp * 128:hp * 128 + 128] = src[hp, 0:rows, :].astype(dst.dtype)


def lane_index(rows):
    return lax.broadcasted_iota(jnp.int32, (rows, 128), 1)


def self_forward(len_ref, hid_ref, gain1_ref, gain2_ref, lag_ref, u_ref,
                 n1_ref, q_ref, k_ref, v_ref, lse_ref, mixed_ref, h1_ref, n2_ref,
                 q_s, k_s, v_s, m_s, bias_s):
    rows = hid_ref.shape[0]
    count = q_ref.shape[0]
    for rb in row_blocks(rows):
        x = hid_ref[rb, :].astype(f32)
        n1_ref[rb, :] = (x * row_scale(x) * gain1_ref[...]).astype(bf16)
    for w, dst in enumerate((q_s, k_s, v_s)):
        for cb in col_blocks():
            put_pairs(dst, cb, rounded(dot(n1_ref[...], weight_cols(u_ref, w, cb))))
        clear_tail(dst, rows)
    starts = starts_of(len_ref)
    row = lax.broadcasted_iota(jnp.int32, (MAX_LEN, MAX_LEN), 0)
    col = lax.broadcasted_iota(jnp.int32, (MAX_LEN, MAX_LEN), 1)
    lane = lane_index(MAX_LEN)
    even = lane < HEAD

    def pair(hp, carry):
        cols = pl.ds(pl.multiple_of(hp * 128, 128), 128)
        for e in range(2):
            w = jnp.broadcast_to(lag_ref[pl.ds(2 * hp + e, 1), :], (MAX_LEN, MAX_LEN))
            table = pltpu.roll(w, 0, 1, stride=1, stride_axis=0)
            bias_s[e] = jnp.where(row >= col, table, masked_score)
        for s in range(count):
            window = pl.ds(starts[s], MAX_LEN)
            q = q_s[hp, window, :].astype(bf16)
            k = k_s[hp, window, :].astype(bf16)
            v = v_s[hp, window, :].astype(bf16)
            q_ref[s, :, cols] = q
            k_ref[s, :, cols] = k
            v_ref[s, :, cols] = v
            res, tops = [], []
            for e in range(2):
                mine = even if e == 0 else ~even
                score = dot_nt(jnp.where(mine, q, 0), k) + bias_s[e]
                top = jnp.max(score, axis=-1, keepdims=True)
                p = jnp.exp(score - top).astype(bf16)
                res.append(dot(p, jnp.where(mine, v, 1)))
                tops.append(top)
            num = jnp.where(even, res[0], res[1])
            den = jnp.where(even, pltpu.roll(res[0], HEAD, 1), pltpu.roll(res[1], HEAD, 1))
            lse_ref[s, :, cols] = jnp.where(even, tops[0], tops[1]) + jnp.log(den)
            m_s[hp, window, :] = num / den
        return carry

    lax.fori_loop(0, PAIRS, pair, 0)
    join_pairs(mixed_ref, m_s, rows)
    for cb in col_blocks():
        h1_ref[:, cb] = hid_ref[:, cb].astype(f32) + dot(mixed_ref[...], weight_cols(u_ref, 3, cb))
    for rb in row_blocks(rows):
        x = h1_ref[rb, :]
        n2_ref[rb, :] = (x * row_scale(x) * gain2_ref[...]).astype(bf16)


def cross_forward(len_ref, n2_ref, h1_ref, gain3_ref, enc_ref, u_ref,
                  ck_ref, cv_ref, cq_ref, lse_ref, crossed_ref, h2_ref, n3_ref,
                  q_s, m_s):
    s = pl.program_id(0)
    rows = n2_ref.shape[0]
    count = pl.num_programs(0)

    @pl.when(s == 0)
    def _():
        for cb in col_blocks():
            put_pairs(q_s, cb, rounded(dot(n2_ref[...], weight_cols(u_ref, 0, cb))))
        clear_tail(q_s, rows)

    for cb in col_blocks():
        ck_ref[:, cb] = dot(enc_ref[...], weight_cols(u_ref, 1, cb)).astype(bf16)
        cv_ref[:, cb] = dot(enc_ref[...], weight_cols(u_ref, 2, cb)).astype(bf16)
    start = 0
    for t in range(3):
        start = start + jnp.where(s > t, len_ref[t], 0)
    window = pl.ds(start, MAX_LEN)
    even = lane_index(MAX_LEN) < HEAD
    even_v = lane_index(ENC_LEN) < HEAD

    def pair(hp, carry):
        cols = pl.ds(pl.multiple_of(hp * 128, 128), 128)
        q = q_s[hp, window, :].astype(bf16)
        cq_ref[0, :, cols] = q
        k = ck_ref[:, cols]
        v = cv_ref[:, cols]
        res, tops = [], []
        for e in range(2):
            mine = even if e == 0 else ~even
            mine_v = even_v if e == 0 else ~even_v
            score = dot_nt(jnp.where(mine, q, 0), k)
            top = jnp.max(score, axis=-1, keepdims=True)
            p = jnp.exp(score - top).astype(bf16)
            res.append(dot(p, jnp.where(mine_v, v, 1)))
            tops.append(top)
        num = jnp.where(even, res[0], res[1])
        den = jnp.where(even, pltpu.roll(res[0], HEAD, 1), pltpu.roll(res[1], HEAD, 1))
        lse_ref[0, :, cols] = jnp.where(even, tops[0], tops[1]) + jnp.log(den)
        m_s[hp, window, :] = num / den
        return carry

    lax.fori_loop(0, PAIRS, pair, 0)

    @pl.when(s == count - 1)
    def _():
        join_pairs(crossed_ref, m_s, rows)
        for cb in col_blocks():
            h2_ref[:, cb] = h1_ref[:, cb] + dot(crossed_ref[...], weight_cols(u_ref, 3, cb))
        for rb in row_blocks(rows):
            x = h2_ref[rb, :]
            n3_ref[rb, :] = (x * row_scale(x) * gain3_ref[...]).astype(bf16)


def gelu_parts(x):
    decay = jnp.exp(-0.5 * (x * x))
    t = 1.0 / (1.0 + jnp.abs(x) * (0.3275911 / math.sqrt(2.0)))
    poly = t * (0.5 * 0.254829592 + t * (-0.5 * 0.284496736 + t * (
        0.5 * 1.421413741 + t * (-0.5 * 1.453152027 + t * (0.5 * 1.061405429)))))
    tail = poly * decay
    below = jnp.where(x >= 0, 1.0 - tail, tail)
    return x * below, below + x * decay * (1.0 / math.sqrt(2.0 * math.pi))


def feed_forward(len_ref, group_ref, step_ref, weight_ref, tags_ref, mask_ref, og_ref, n3_ref,
                 h2_ref, gain3_ref, x_ref, r_ref,
                 out_ref, gx_ref, gr_ref, g2_ref, gg_ref,
                 scaled_s, out_s, dn_s, act_s, de_s):
    g = pl.program_id(0)
    rows = n3_ref.shape[0]

    def token_weight(rb):
        index = lax.broadcasted_iota(jnp.int32, (128, 1), 0) + rb.start
        scale = jnp.zeros((128, 1), f32)
        tagged = jnp.zeros((128, 1), jnp.int32)
        start = 0
        for s in range(4):
            group = group_ref[s]
            factor = jnp.float32(0.0)
            for k in range(GROUPS):
                value = weight_ref[k].astype(f32) * 0.25 * (
                    1.0 - step_ref[k].astype(f32) * (1.0 / (2.0 * HORIZON)))
                factor = jnp.where(group == k, value, factor)
            inside = index >= start
            scale = jnp.where(inside, factor, scale)
            tagged = jnp.where(inside, jnp.where(group == 1, 1, 0), tagged)
            start = start + len_ref[s]
        counted = jnp.where(tagged == 1, tags_ref[rb, :], mask_ref[rb, :]).astype(f32)
        return scale * (0.25 + 0.75 * counted)

    @pl.when(g == 0)
    def _():
        for rb in row_blocks(rows):
            scaled = og_ref[rb, :].astype(f32) * token_weight(rb)
            g2_ref[rb, :] = scaled
            scaled_s[rb, :] = scaled.astype(bf16)
        out_s[...] = h2_ref[...]
        dn_s[...] = jnp.zeros(dn_s.shape, f32)

    for cb in col_blocks():
        expanded = dot(n3_ref[...], x_ref[:, 0, :, cb].reshape(D, COLS))
        act, slope = gelu_parts(expanded)
        act_s[:, cb] = act.astype(bf16)
        back = dot_nt(scaled_s[...], r_ref[0, cb, :])
        de_s[:, cb] = (back * slope).astype(bf16)
    for cb in col_blocks():
        out_s[:, cb] += dot(act_s[...], r_ref[0, :, cb])
        gx_ref[:, 0, :, cb] = dot_tn(n3_ref[...], de_s[:, cb]).astype(bf16).reshape(4, D // 4, COLS)
        gr_ref[0, :, cb] = dot_tn(act_s[...], scaled_s[:, cb]).astype(bf16)
    full = x_ref[:, 0].reshape(D, D)
    for cb in col_blocks():
        dn_s[:, cb] += dot_nt(de_s[...], full[cb, :])

    @pl.when(g == pl.num_programs(0) - 1)
    def _():
        total = jnp.zeros((1, D), f32)
        for rb in row_blocks(rows):
            out_ref[rb, :] = out_s[rb, :].astype(bf16)
            part, pulled = norm_back(dn_s[rb, :], h2_ref[rb, :], gain3_ref[...])
            g2_ref[rb, :] += part
            total = total + jnp.sum(pulled, axis=0, keepdims=True)
        gg_ref[...] = total


def head_sums(product):
    a = lax.broadcasted_iota(jnp.int32, (128, 128), 0) < HEAD
    b = lax.broadcasted_iota(jnp.int32, (128, 128), 1) < HEAD
    ones = (a == b).astype(bf16)
    high, mid, rest = split_three(product)
    return dot(high, ones) + dot(mid, ones) + dot(rest, ones)


def augment(base, minus, lane, e):
    mine = (lane < HEAD) if e == 0 else (lane >= HEAD)
    spot = HEAD if e == 0 else 0
    high, mid, rest = split_three(-minus)
    extra = jnp.where(lane == spot, high, jnp.where(lane == spot + 1, mid, jnp.where(
        lane == spot + 2, rest, jnp.zeros_like(high))))
    return jnp.where(mine, base, extra)


def ones_beside(base, lane, e):
    mine = (lane < HEAD) if e == 0 else (lane >= HEAD)
    return jnp.where(mine, base, 1)


def other_half(value):
    return pltpu.roll(value, HEAD, 1)


def cross_backward(len_ref, g2_ref, crossed_ref, cq_ref, lse_ref, ck_ref, cv_ref, enc_ref, n2_ref,
                   h1_ref, gain2_ref, u_ref,
                   ge_ref, gu_ref, g1_ref, gg_ref,
                   dm_s, dd_s, dq_s, dk_s, dv_s, gk_s, gv_s, b2_s, dml_s, dn_s):
    s = pl.program_id(0)
    rows = g2_ref.shape[0]

    @pl.when(s == 0)
    def _():
        b2_s[...] = g2_ref[...].astype(bf16)
        full = weight_of(u_ref, 3)
        for cb in col_blocks():
            put_pairs(dm_s, cb, rounded(dot_nt(b2_s[...], full[cb, :])))
            gu_ref[:, 3, :, cb] = dot_tn(crossed_ref[...], b2_s[:, cb]).astype(bf16).reshape(
                4, D // 4, COLS)
        clear_tail(dm_s, rows)
        clear_tail(dd_s, rows)
        for hp in range(PAIRS):
            cols = slice(hp * 128, hp * 128 + 128)
            dd_s[hp, 0:rows, :] = head_sums(dm_s[hp, 0:rows, :] * crossed_ref[:, cols].astype(f32))
        gk_s[...] = jnp.zeros(gk_s.shape, f32)
        gv_s[...] = jnp.zeros(gv_s.shape, f32)

    start = 0
    length = len_ref[0]
    for t in range(3):
        start = start + jnp.where(s > t, len_ref[t], 0)
        length = jnp.where(s == t + 1, len_ref[t + 1], length)
    lane = lane_index(MAX_LEN)
    lane_k = lane_index(ENC_LEN)
    valid = lax.broadcasted_iota(jnp.int32, (MAX_LEN, 128), 0) < length
    window = pl.ds(start, MAX_LEN)

    def pair(hp, carry):
        cols = pl.ds(pl.multiple_of(hp * 128, 128), 128)
        q = cq_ref[0, :, cols]
        k = ck_ref[:, cols]
        v = cv_ref[:, cols]
        lse = other_half(lse_ref[0, :, cols])
        dm = jnp.where(valid, dm_s[hp, window, :], 0.0).astype(bf16)
        dd = other_half(jnp.where(valid, dd_s[hp, window, :], 0.0))
        dq = dk = dv = None
        for e in range(2):
            score = dot_nt(ones_beside(k, lane_k, e), augment(q, lse, lane, e))
            p = jnp.exp(score)
            back = dot_nt(ones_beside(v, lane_k, e), augment(dm, dd, lane, e))
            ds = (p * back).astype(bf16)
            mine = (lane < HEAD) if e == 0 else (lane >= HEAD)
            mine_k = (lane_k < HEAD) if e == 0 else (lane_k >= HEAD)
            dv_e = dot(p.astype(bf16), jnp.where(mine, dm, 0))
            dk_e = dot(ds, jnp.where(mine, q, 0))
            dq_e = dot_tn(ds, jnp.where(mine_k, k, 0))
            dq, dk, dv = (dq_e, dk_e, dv_e) if e == 0 else (dq + dq_e, dk + dk_e, dv + dv_e)
        dq_s[hp, window, :] = dq
        dk_s[:, cols] = dk.astype(bf16)
        dv_s[:, cols] = dv.astype(bf16)
        return carry

    lax.fori_loop(0, PAIRS, pair, 0)
    full_k = weight_of(u_ref, 1)
    full_v = weight_of(u_ref, 2)
    for cb in col_blocks():
        gk_s[:, cb] += dot_tn(enc_ref[...], dk_s[:, cb])
        gv_s[:, cb] += dot_tn(enc_ref[...], dv_s[:, cb])
        ge_ref[:, cb] = dot_nt(dk_s[...], full_k[cb, :]) + dot_nt(dv_s[...], full_v[cb, :])

    @pl.when(s == pl.num_programs(0) - 1)
    def _():
        join_pairs(dml_s, dq_s, rows)
        full_q = weight_of(u_ref, 0)
        for cb in col_blocks():
            gu_ref[:, 0, :, cb] = dot_tn(n2_ref[...], dml_s[:, cb]).astype(bf16).reshape(
                4, D // 4, COLS)
            gu_ref[:, 1, :, cb] = gk_s[:, cb].astype(bf16).reshape(4, D // 4, COLS)
            gu_ref[:, 2, :, cb] = gv_s[:, cb].astype(bf16).reshape(4, D // 4, COLS)
            dn_s[:, cb] = dot_nt(dml_s[...], full_q[cb, :])
        total = jnp.zeros((1, D), f32)
        for rb in row_blocks(rows):
            part, pulled = norm_back(dn_s[rb, :], h1_ref[rb, :], gain2_ref[...])
            g1_ref[rb, :] = g2_ref[rb, :] + part
            total = total + jnp.sum(pulled, axis=0, keepdims=True)
        gg_ref[...] = total


def diagonal_sums(ref):
    total = ref[0:8, :]
    for r in range(8, MAX_LEN, 8):
        total = total + pltpu.roll(ref[r:r + 8, :], MAX_LEN - r, 1)
    row = lax.broadcasted_iota(jnp.int32, (8, MAX_LEN), 0)
    for bit in (1, 2, 4):
        total = jnp.where((row & bit) != 0, pltpu.roll(total, MAX_LEN - bit, 1), total)
    return jnp.sum(total, axis=0, keepdims=True)


def self_backward(len_ref, g1_ref, mixed_ref, q_ref, k_ref, v_ref, lse_ref, n1_ref, hid_ref,
                  gain1_ref, lag_ref, u_ref,
                  gh_ref, gu_ref, gg_ref, gl_ref,
                  dm_s, dd_s, dq_s, dk_s, dv_s, b1_s, low_s, bias_s, acc_s, dn_s):
    rows = g1_ref.shape[0]
    count = q_ref.shape[0]
    b1_s[...] = g1_ref[...].astype(bf16)
    full = weight_of(u_ref, 3)
    for cb in col_blocks():
        put_pairs(dm_s, cb, rounded(dot_nt(b1_s[...], full[cb, :])))
        gu_ref[:, 3, :, cb] = dot_tn(mixed_ref[...], b1_s[:, cb]).astype(bf16).reshape(
            4, D // 4, COLS)
    clear_tail(dm_s, rows)
    clear_tail(dd_s, rows)
    for hp in range(PAIRS):
        cols = slice(hp * 128, hp * 128 + 128)
        dd_s[hp, 0:rows, :] = head_sums(dm_s[hp, 0:rows, :] * mixed_ref[:, cols].astype(f32))
    starts = starts_of(len_ref)
    row = lax.broadcasted_iota(jnp.int32, (MAX_LEN, MAX_LEN), 0)
    col = lax.broadcasted_iota(jnp.int32, (MAX_LEN, MAX_LEN), 1)
    lane = lane_index(MAX_LEN)
    index = lax.broadcasted_iota(jnp.int32, (MAX_LEN, 128), 0)

    def pair(hp, carry):
        cols = pl.ds(pl.multiple_of(hp * 128, 128), 128)
        for e in range(2):
            w = jnp.broadcast_to(lag_ref[pl.ds(2 * hp + e, 1), :], (MAX_LEN, MAX_LEN))
            table = pltpu.roll(w, 0, 1, stride=1, stride_axis=0)
            bias_s[e] = jnp.where(col >= row, table, masked_score)
        for s in range(count):
            valid = index < len_ref[s]
            window = pl.ds(starts[s], MAX_LEN)
            q = q_ref[s, :, cols]
            k = k_ref[s, :, cols]
            v = v_ref[s, :, cols]
            lse = other_half(lse_ref[s, :, cols])
            dm = jnp.where(valid, dm_s[hp, window, :], 0.0).astype(bf16)
            dd = other_half(jnp.where(valid, dd_s[hp, window, :], 0.0))
            dq = dk = dv = None
            for e in range(2):
                score = dot_nt(ones_beside(k, lane, e), augment(q, lse, lane, e)) + bias_s[e]
                p = jnp.exp(score)
                back = dot_nt(ones_beside(v, lane, e), augment(dm, dd, lane, e))
                grad = p * back
                if s == 0:
                    acc_s[e] = grad
                else:
                    acc_s[e] += grad
                ds = grad.astype(bf16)
                mine = (lane < HEAD) if e == 0 else (lane >= HEAD)
                dv_e = dot(p.astype(bf16), jnp.where(mine, dm, 0))
                dk_e = dot(ds, jnp.where(mine, q, 0))
                dq_e = dot_tn(ds, jnp.where(mine, k, 0))
                dq, dk, dv = (dq_e, dk_e, dv_e) if e == 0 else (dq + dq_e, dk + dk_e, dv + dv_e)
            dq_s[hp, window, :] = dq
            dk_s[hp, window, :] = dk
            dv_s[hp, window, :] = dv
        for e in range(2):
            gl_ref[pl.ds(2 * hp + e, 1), :] = diagonal_sums(acc_s.at[e])
        return carry

    lax.fori_loop(0, PAIRS, pair, 0)
    for w, src in enumerate((dq_s, dk_s, dv_s)):
        join_pairs(low_s, src, rows)
        full = weight_of(u_ref, w)
        for cb in col_blocks():
            gu_ref[:, w, :, cb] = dot_tn(n1_ref[...], low_s[:, cb]).astype(bf16).reshape(
                4, D // 4, COLS)
            part = dot_nt(low_s[...], full[cb, :])
            dn_s[:, cb] = part if w == 0 else dn_s[:, cb] + part
    total = jnp.zeros((1, D), f32)
    for rb in row_blocks(rows):
        part, pulled = norm_back(dn_s[rb, :], hid_ref[rb, :].astype(f32), gain1_ref[...])
        gh_ref[rb, :] = g1_ref[rb, :] + part
        total = total + jnp.sum(pulled, axis=0, keepdims=True)
    gg_ref[...] = total


def bucket_table():
    lags = np.arange(MAX_LEN)
    exact = BUCKETS // 2
    bucket = np.minimum(lags, exact)
    for step in range(1, exact):
        edge = math.ceil(exact * (MAX_DIST / exact) ** (step / exact))
        bucket = bucket + (lags >= edge)
    return (bucket[None, :] == np.arange(BUCKETS)[:, None]).astype(np.float32)


def shape(dims, kind):
    return jax.ShapeDtypeStruct(dims, kind)


def call(kernel, name, outs, ins, scratch, **extra):
    return pl.pallas_call(
        kernel,
        out_shape=list(outs),
        name=name,
        scratch_shapes=scratch,
        compiler_params=pltpu.CompilerParams(vmem_limit_bytes=LIMIT),
        **extra,
    )(*ins)


def whole(array_shape):
    zeros = (0,) * len(array_shape)
    return pl.BlockSpec(array_shape, lambda s: zeros)


def gather_unit(unit):
    parts = lax.axis_size("dp")
    size = D // parts
    piece = lax.dynamic_slice_in_dim(unit, lax.axis_index("dp") * size, size, 0)
    return lax.all_gather(piece, ("fsdp", "dp"), axis=0, tiled=True).reshape(4, 4, D // 4, D)


def reduce_unit(grads):
    return lax.psum_scatter(
        grads.reshape(4 * D, D), ("fsdp", "dp"), scatter_dimension=0, tiled=True)


def per_device(
    hidden, encoded, out_grad, lengths, group_ids, id_tags, loss_mask, group_steps, group_weights,
    gain_self, gain_cross, gain_ffn, rel_bias,
    query_weight, key_weight, value_weight, output_weight,
    cross_query, cross_key, cross_value, cross_output, expand_weight, reduce_weight,
):
    rows = hidden.shape[0]
    count = lengths.shape[0]
    quarter = D // 4
    u_self = gather_unit(jnp.concatenate([query_weight, key_weight, value_weight, output_weight], 0))
    small = jnp.concatenate([gain_self, gain_cross, gain_ffn, rel_bias.reshape(-1)])
    small = lax.all_gather(small[None], "fsdp", axis=0, tiled=True).astype(f32)
    u_cross = gather_unit(jnp.concatenate([cross_query, cross_key, cross_value, cross_output], 0))
    u_x = gather_unit(
        jnp.concatenate([expand_weight[:, g * D:(g + 1) * D] for g in range(4)], 0))
    u_r = gather_unit(reduce_weight)

    gain1 = small[:, 0:quarter].reshape(1, D)
    gain2 = small[:, quarter:2 * quarter].reshape(1, D)
    gain3 = small[:, 2 * quarter:3 * quarter].reshape(1, D)
    rel = small[:, 3 * quarter:].reshape(HEADS, BUCKETS)
    table = bucket_table()
    by_lag = jnp.dot(rel, jnp.asarray(table), precision=lax.Precision.HIGHEST)
    turned = jnp.dot(
        rel, jnp.asarray(table[:, (-np.arange(MAX_LEN)) % MAX_LEN]), precision=lax.Precision.HIGHEST)

    pad = rows + MAX_LEN
    wide = pltpu.VMEM((PAIRS, pad, 128), f32)
    heads = (count, MAX_LEN, D)
    n1, q, k, v, lse, mixed, h1, n2 = call(
        self_forward, "self_forward",
        (shape((rows, D), bf16), shape(heads, bf16), shape(heads, bf16), shape(heads, bf16),
         shape(heads, f32), shape((rows, D), bf16), shape((rows, D), f32), shape((rows, D), bf16)),
        (lengths, hidden, gain1, gain2, turned, u_self),
        [wide, wide, wide, wide, pltpu.VMEM((2, MAX_LEN, MAX_LEN), f32)],
        in_specs=[SMEM] + [VMEM] * 5, out_specs=[VMEM] * 8)

    enc_block = pl.BlockSpec((ENC_LEN, D), lambda s: (s, 0))
    seq_block = pl.BlockSpec((1, MAX_LEN, D), lambda s: (s, 0, 0))
    unit = whole((4, 4, quarter, D))
    full = whole((rows, D))
    line = whole((1, D))
    ck, cv, cq, cross_lse, crossed, h2, n3 = call(
        cross_forward, "cross_forward",
        (shape(encoded.shape, bf16), shape(encoded.shape, bf16), shape(heads, bf16),
         shape(heads, f32), shape((rows, D), bf16), shape((rows, D), f32), shape((rows, D), bf16)),
        (lengths, n2, h1, gain3, encoded, u_cross),
        [wide, wide],
        grid=(count,),
        in_specs=[SMEM, full, full, line, enc_block, unit],
        out_specs=[enc_block, enc_block, seq_block, seq_block, full, full, full])

    column = whole((rows, 1))
    x_block = pl.BlockSpec((4, 1, quarter, D), lambda g: (0, g, 0, 0))
    r_block = pl.BlockSpec((1, D, D), lambda g: (g, 0, 0))
    low = pltpu.VMEM((rows, D), bf16)
    flat = pltpu.VMEM((rows, D), f32)
    layer_output, grad_x, grad_r, g2, gg3 = call(
        feed_forward, "feed_forward",
        (shape((rows, D), bf16), shape((4, 4, quarter, D), bf16), shape((4, D, D), bf16),
         shape((rows, D), f32), shape((1, D), f32)),
        (lengths, group_ids, group_steps, group_weights, id_tags[:, None], loss_mask[:, None],
         out_grad, n3, h2, gain3, u_x, u_r.reshape(4, D, D)),
        [low, flat, flat, low, low],
        grid=(4,),
        in_specs=[SMEM] * 4 + [column, column, full, full, full, line, x_block, r_block],
        out_specs=[full, x_block, r_block, full, line])
    piece_x = reduce_unit(grad_x)
    piece_r = reduce_unit(grad_r)

    grad_encoded, grad_cross, g1, gg2 = call(
        cross_backward, "cross_backward",
        (shape(encoded.shape, f32), shape((4, 4, quarter, D), bf16), shape((rows, D), f32),
         shape((1, D), f32)),
        (lengths, g2, crossed, cq, cross_lse, ck, cv, encoded, n2, h1, gain2, u_cross),
        [wide, wide, wide, pltpu.VMEM((ENC_LEN, D), bf16), pltpu.VMEM((ENC_LEN, D), bf16),
         pltpu.VMEM((D, D), f32), pltpu.VMEM((D, D), f32), low, low, flat],
        grid=(count,),
        in_specs=[SMEM, full, full, seq_block, seq_block, enc_block, enc_block, enc_block, full,
                  full, line, unit],
        out_specs=[enc_block, unit, full, line])
    piece_cross = reduce_unit(grad_cross)

    grad_hidden, grad_self, gg1, grad_lag = call(
        self_backward, "self_backward",
        (shape((rows, D), f32), shape((4, 4, quarter, D), bf16), shape((1, D), f32),
         shape((HEADS, MAX_LEN), f32)),
        (lengths, g1, mixed, q, k, v, lse, n1, hidden, gain1, by_lag, u_self),
        [wide, wide, wide, wide, wide, low, low,
         pltpu.VMEM((2, MAX_LEN, MAX_LEN), f32), pltpu.VMEM((2, MAX_LEN, MAX_LEN), f32), flat],
        in_specs=[SMEM] + [VMEM] * 11, out_specs=[VMEM] * 4)
    piece_self = reduce_unit(grad_self)

    grad_rel = lax.dot_general(
        grad_lag, jnp.asarray(table), (((1,), (1,)), ((), ())), precision=lax.Precision.HIGHEST)
    small_grads = jnp.concatenate(
        [gg1.reshape(4, quarter), gg2.reshape(4, quarter), gg3.reshape(4, quarter),
         grad_rel.reshape(4, -1)], axis=1)
    small_total = lax.psum(small_grads, ("dp", "fsdp"))
    small_mine = lax.dynamic_slice_in_dim(small_total, lax.axis_index("fsdp"), 1, 0)[0]

    pieces = jnp.stack([piece_self, piece_cross, piece_x, piece_r])
    shards = lax.all_gather(pieces, "dp", axis=1, tiled=True).astype(f32)
    blocks = shards.reshape(4, 4, quarter, D)
    return (
        layer_output,
        grad_hidden,
        grad_encoded,
        small_mine[0:quarter],
        small_mine[quarter:2 * quarter],
        small_mine[2 * quarter:3 * quarter],
        small_mine[3 * quarter:].reshape(HEADS // 4, BUCKETS),
        blocks[0, 0],
        blocks[0, 1],
        blocks[0, 2],
        blocks[0, 3],
        blocks[1, 0],
        blocks[1, 1],
        blocks[1, 2],
        blocks[1, 3],
        jnp.concatenate([blocks[2, g] for g in range(4)], axis=1),
        shards[3],
    )


def solution(mesh):
    rows = P(("dp", "fsdp"), None)
    flat = P(("dp", "fsdp"))
    shard = P("fsdp", None)
    line = P("fsdp")
    return jax.shard_map(
        per_device,
        mesh=mesh,
        in_specs=(rows, rows, rows, flat, flat, flat, flat, P(), P(), line, line, line) + (shard,) * 11,
        out_specs=(rows, rows, rows, line, line, line) + (shard,) * 11,
        check_vma=False,
    )
```

time: 1460 us -> 901 us (0.62)
  local copies, waits for them, and re-layouts: 351 us -> 11.3 us
  matrix products: 297 us -> 1.61 us
  Pallas kernels: 0 us -> 170 us
  other arithmetic: 98.2 us -> 11.7 us
    dot_general x62 -> x3, matrix products: 297 us -> 1.61 us  [the longest x1 0.74 us: per_device(): jnp.dot(rel, jnp.asarray(table[:, -np.arange(MAX_LEN) % MAX_LEN]), precis...]
    pallas_call x0 -> x5, Pallas kernels: none -> 170 us  [call(): pl.pallas_call(kernel, out_shape=list(outs), name=name, scratch_shapes=sc...]
    unnamed x315 -> x35, local copies, waits for them, and re-layouts: 101 us -> 0.89 us
    reshape x11 -> x10, local copies, waits for them, and re-layouts: 101 us -> 3.14 us  [the longest x1 0.67 us: per_device(): gain3 = small[:, 2 * quarter:3 * quarter].reshape(1, D)]
    all_gather x10 -> x5, waiting for transfers between devices: 102 us -> 192 us  [the longest x4 192 us: gather_unit(): lax.all_gather(piece, ('fsdp', 'dp'), axis=0, tiled=True)]
    reduce_scatter x8 -> x4, waiting for transfers between devices: 514 us -> 438 us  [reduce_unit(): lax.psum_scatter(grads.reshape(4 * D, D), ('fsdp', 'dp'), scatter_dimensi...]
    another operation x4 -> x0, local copies, waits for them, and re-layouts: 47.3 us -> none  [the longest x2 43.9 us: distance_bias(): jnp.tile(period, (1, rows))[:, :rows * rows].reshape(heads, rows, rows)]
    reduce_sum x10 -> x0, other arithmetic: 28.8 us -> none  [the longest x5 15.5 us: softmax_parts(): total = jnp.sum(powers, axis=-1, keepdims=True)]
  transfers between devices with their start and end apart: 21 -> 9, of which waited for: 8 -> 8; matrix products, arithmetic and copies ran while one was open for 44% -> 1% of each run, Pallas kernels for 0% -> 6%
where the time goes in v1:
time: 901 us; the launch traced here: 890 us
  waiting for transfers between devices  631 us (70%)
  Pallas kernels  170 us (19%)
  blocking collectives  48.2 us (5%)
  between operations  15.2 us (2%)
  other arithmetic  11.7 us (1%)
  local copies, waits for them, and re-layouts  11.3 us (1%)
    reduce_scatter x4, waiting for transfers between devices, reduce_unit(): lax.psum_scatter(grads.reshape(4 * D, D), ('fsdp', 'dp'), scatter_dimensi...  438 us
    all_gather x4, waiting for transfers between devices, gather_unit(): lax.all_gather(piece, ('fsdp', 'dp'), axis=0, tiled=True)  192 us
    pallas_call x5, Pallas kernels, call(): pl.pallas_call(kernel, out_shape=list(outs), name=name, scratch_shapes=sc...  170 us
    psum x1, blocking collectives, per_device(): small_total = lax.psum(small_grads, ('dp', 'fsdp'))  40.9 us
  transfers between devices with their start and end apart: 9, of which 8 were waited for; matrix products, arithmetic and copies ran while one was open for 1% of the time, Pallas kernels for 6%

profile of v1, /device:TPU:9, one launch (start us, length us, event | category | flops | bytes accessed | tf_op | source)
XLA Modules:
  0.0 890.0 jit_solution(14403073241502378719)
XLA Ops:
  7.3 1.9 fusion.8
  9.3 1.8 fusion.5
  11.3 1.0 fusion.2
  12.3 0.7 constant_dynamic-slice_fusion.1
  14.7 7.3 all-reduce
  22.3 0.7 reshape.94.gain1_ref
  23.7 0.7 reshape.98.gain3_ref
  24.4 0.9 broadcast_in_dim.12.tags_ref
  25.2 0.9 broadcast_in_dim.13.mask_ref
  26.1 0.7 fusion.12.lag_ref
  26.9 0.7 fusion.13.lag_ref
  27.6 49.6 %all-gather.7.cloned.1.call-done = bf16[3072,768]{1,0:T(8,128)(2,1)} async-done(((bf16[96,768]{1,0:T(8,128)(2,1)}), bf16[3072,768]{1,0:T(8,128)(2,1)}) %all-gather.7.cloned.1.call-update) | async-done | bytes 4718608 | tf_op jit(solution)/shard_map/all_gather | solution.py:523
  77.2 21.4 %self_forward.1 = (bf16[640,768]{1,0:T(8,128)(2,1)}, bf16[4,256,768]{2,1,0:T(8,128)(2,1)}, bf16[4,256,768]{2,1,0:T(8,128)(2,1)}, bf16[4,256,768]{2,1,0:T(8,128)(...) custom-call(s32[4]{0:T(128)} %len_ref.9, ...), custom_call_target="tpu_custom_call" | custom-call | tf_op jit(solution)/shard_map/self_forward/pallas_call | solution.py:504
  98.7 44.5 %all-gather.9.cloned.1.call-done = bf16[3072,768]{1,0:T(8,128)(2,1)} async-done(((bf16[96,768]{1,0:T(8,128)(2,1)}), bf16[3072,768]{1,0:T(8,128)(2,1)}) %all-gather.9.cloned.1.call-update) | async-done | bytes 4718608 | tf_op jit(solution)/shard_map/all_gather | solution.py:523
  143.2 34.2 %cross_forward.1 = (bf16[2048,768]{1,0:T(8,128)(2,1)}, bf16[2048,768]{1,0:T(8,128)(2,1)}, bf16[4,256,768]{2,1,0:T(8,128)(2,1)}, f32[4,256,768]{2,1,0:T(8,128)}, ...) custom-call(s32[4]{0:T(128)} %len_ref.9, bf16[640,768]{1,0:T(8,128)(2,1)} %get-tuple-element.45.n2_ref, ...), custom_call_target="tpu_custom_call" | custom-call | tf_op jit(solution)/shard_map/cross_forward/pallas_call | solution.py:504
  177.4 31.8 %all-gather.11.cloned.1.call-done = bf16[3072,768]{1,0:T(8,128)(2,1)} async-done(((bf16[96,768]{1,0:T(8,128)(2,1)}), bf16[3072,768]{1,0:T(8,128)(2,1)}) %all-gather.11.cloned.1.call-update) | async-done | bytes 4718608 | tf_op jit(solution)/shard_map/all_gather | solution.py:523
  209.2 65.8 %all-gather.13.cloned.1.call-done = bf16[3072,768]{1,0:T(8,128)(2,1)} async-done(((bf16[96,768]{1,0:T(8,128)(2,1)}), bf16[3072,768]{1,0:T(8,128)(2,1)}) %all-gather.13.cloned.1.call-update) | async-done | bytes 4718608 | tf_op jit(solution)/shard_map/all_gather | solution.py:523
  275.0 31.9 %feed_forward.1 = (bf16[640,768]{1,0:T(8,128)(2,1)}, bf16[4,4,192,768]{3,2,1,0:T(8,128)(2,1)}, bf16[4,768,768]{2,1,0:T(8,128)(2,1)}, f32[640,768]{1,0:T(8,128)}, f32[1,768]{1,0:T(1,128)}) custom-call(s32[4]{0:T(128)} %len_ref.9, s32[4]{0:T(128)} %group_ref.1, s32[3]{0:T(128)} %step_ref.1, s32[3]{0:T(128)} %weight_ref.1, s32[640,1]{1,0:T(8,128)} %broadcast_in_dim.12.tags_ref, ...), custom_call_target="tpu_custom_call" | custom-call | tf_op jit(solution)/shard_map/feed_forward/pallas_call | solution.py:504
  306.9 50.7 %cross_backward.1 = (f32[2048,768]{1,0:T(8,128)}, bf16[4,4,192,768]{3,2,1,0:T(8,128)(2,1)}, f32[640,768]{1,0:T(8,128)}, f32[1,768]{1,0:T(1,128)}) custom-call(s32[4]{0:T(128)} %len_ref.9, f32[640,768]{1,0:T(8,128)} %get-tuple-element.50.g2_ref, bf16[640,768]{1,0:T(8,128)(2,1)} %get-tuple-element.51.crossed_ref, ...), custom_call_target="tpu_custom_call" | custom-call | tf_op jit(solution)/shard_map/cross_backward/pallas_call | solution.py:504
  357.5 32.2 %self_backward.1 = (f32[640,768]{1,0:T(8,128)}, bf16[4,4,192,768]{3,2,1,0:T(8,128)(2,1)}, f32[1,768]{1,0:T(1,128)}, f32[12,256]{1,0:T(8,128)}) custom-call(s32[4]{0:T(128)} %len_ref.9, f32[640,768]{1,0:T(8,128)} %get-tuple-element.56.g1_ref, bf16[640,768]{1,0:T(8,128)(2,1)} %get-tuple-element.57.mixed_ref, bf16[4,256,768]{2,1,0:T(8,128)(2,1)} %get-tuple-element.58.q_ref, ...), custom_call_target="tpu_custom_call" | custom-call | tf_op jit(solution)/shard_map/self_backward/pallas_call | solution.py:504
  390.4 0.7 reduce-scatter.9.cloned.1.call-update
  391.9 101.1 %reduce-scatter.5.cloned.1.call-done = bf16[96,768]{1,0:T(8,128)(2,1)} async-done(((bf16[3072,768]{1,0:T(8,128)(2,1)}), bf16[96,768]{1,0:T(8,128)(2,1)}) %reduce-scatter.5.cloned.1.call-update) | async-done | bytes 147472 | tf_op jit(solution)/shard_map/reduce_scatter | solution.py:527
  493.0 112.4 %reduce-scatter.7.cloned.1.call-done = bf16[96,768]{1,0:T(8,128)(2,1)} async-done(((bf16[3072,768]{1,0:T(8,128)(2,1)}), bf16[96,768]{1,0:T(8,128)(2,1)}) %reduce-scatter.7.cloned.1.call-update) | async-done | bytes 147472 | tf_op jit(solution)/shard_map/reduce_scatter | solution.py:527
  605.4 111.6 %reduce-scatter.9.cloned.1.call-done = bf16[96,768]{1,0:T(8,128)(2,1)} async-done(((bf16[3072,768]{1,0:T(8,128)(2,1)}), bf16[96,768]{1,0:T(8,128)(2,1)}) %reduce-scatter.9.cloned.1.call-update) | async-done | bytes 147472 | tf_op jit(solution)/shard_map/reduce_scatter | solution.py:527
  717.0 112.5 %reduce-scatter.11.cloned.1.call-done = bf16[96,768]{1,0:T(8,128)(2,1)} async-done(((bf16[3072,768]{1,0:T(8,128)(2,1)}), bf16[96,768]{1,0:T(8,128)(2,1)}) %reduce-scatter.11.cloned.1.call-update) | async-done | bytes 147472 | tf_op jit(solution)/shard_map/reduce_scatter | solution.py:527
  829.5 2.0 pad_maximum_fusion.1
  832.2 40.9 %psum.7 = f32[4,672]{1,0:T(4,128)S(1)} all-reduce(f32[4,672]{1,0:T(4,128)S(1)} %pad_maximum_fusion.2), channel_id=1, replica_groups=mesh['dp'=8,'fsdp'=4] {'dp','fsdp'}, use_global_device_ids=true, to_apply=%region_0.0 | all-reduce | flops 2688 | bytes 21504 | tf_op jit(solution)/shard_map/psum | solution.py:629
  873.2 0.7 reshape.105
  874.5 3.2 convert_element_type.7
  877.6 1.6 slice_bitcast_fusion
  879.2 2.2 slice_bitcast_fusion.4
  881.4 1.7 pad_maximum_fusion
  (72 shorter events, 5.1 us)
Async XLA Ops:
  7.2 5.1 copy-start
  7.2 4.0 copy-start.2
  7.2 70.0 %all-gather.7.cloned.1.call-start = ((), (), s32[]{:S(2)}) async-start(), calls=%async_computation.4 | async-start | bytes 4866048 | tf_op jit(solution)/shard_map/all_gather | solution.py:523
  9.2 134.0 %all-gather.9.cloned.1.call-start = ((), (), s32[]{:S(2)}) async-start(), calls=%async_computation.5 | async-start | bytes 4866048 | tf_op jit(solution)/shard_map/all_gather | solution.py:523
  11.0 2.0 copy-start.14
  11.0 2.1 copy-start.15
  11.0 3.4 copy-start.11
  11.0 3.4 copy-start.12
  11.0 3.4 copy-start.13
  11.1 13.3 %copy-start.6 = (s32[640]{0:T(1024)S(1)}, s32[640]{0:T(1024)}, u32[]{:S(2)}) copy-start(s32[640]{0:T(1024)} %param.30) | copy-start | bytes 7684
  11.1 14.1 %copy-start.7 = (s32[640]{0:T(1024)S(1)}, s32[640]{0:T(1024)}, u32[]{:S(2)}) copy-start(s32[640]{0:T(1024)} %param.31) | copy-start | bytes 7684
  11.1 15.0 %copy-start.4 = (f32[32,256]{1,0:T(8,128)S(1)}, f32[32,256]{1,0:T(8,128)}, u32[]{:S(2)}) copy-start(f32[32,256]{1,0:T(8,128)} %constant.22.clone) | copy-start | bytes 98308
  11.1 15.7 %copy-start.3 = (f32[32,256]{1,0:T(8,128)S(1)}, f32[32,256]{1,0:T(8,128)}, u32[]{:S(2)}) copy-start(f32[32,256]{1,0:T(8,128)} %constant.21.clone) | copy-start | bytes 98308
  11.1 198.0 %all-gather.11.cloned.1.call-start = ((), (), s32[]{:S(2)}) async-start(), calls=%async_computation.6 | async-start | bytes 4866048 | tf_op jit(solution)/shard_map/all_gather | solution.py:523
  12.3 262.7 %all-gather.13.cloned.1.call-start = ((), (), s32[]{:S(2)}) async-start(), calls=%async_computation.7 | async-start | bytes 4866048 | tf_op jit(solution)/shard_map/all_gather | solution.py:523
  13.0 480.0 %reduce-scatter.5.cloned.1.call-start = ((), (), s32[]{:S(2)}) async-start(), calls=%async_computation.8 | async-start | bytes 4866048 | tf_op jit(solution)/shard_map/reduce_scatter | solution.py:527
  389.7 215.7 %reduce-scatter.7.cloned.1.call-start = ((), (), s32[]{:S(2)}) async-start(), calls=%async_computation.9 | async-start | bytes 4866048 | tf_op jit(solution)/shard_map/reduce_scatter | solution.py:527
  390.3 326.7 %reduce-scatter.9.cloned.1.call-start = ((), (), s32[]{:S(2)}) async-start(), calls=%async_computation.10 | async-start | bytes 4866048 | tf_op jit(solution)/shard_map/reduce_scatter | solution.py:527
  391.1 438.4 %reduce-scatter.11.cloned.1.call-start = ((), (), s32[]{:S(2)}) async-start(), calls=%async_computation.11 | async-start | bytes 4866048 | tf_op jit(solution)/shard_map/reduce_scatter | solution.py:527
  391.1 440.4 %copy-start.5 = (f32[12,256]{1,0:T(8,128)S(1)}, f32[12,256]{1,0:T(8,128)}, u32[]{:S(2)}) copy-start(f32[12,256]{1,0:T(8,128)} %get-tuple-element.68) | copy-start | bytes 36868
  391.1 440.6 %copy-start.10 = (f32[1,768]{1,0:T(1,128)S(1)}, f32[1,768]{1,0:T(1,128)}, u32[]{:S(2)}) copy-start(f32[1,768]{1,0:T(1,128)} %get-tuple-element.65) | copy-start | bytes 9220
  391.1 440.7 %copy-start.9 = (f32[1,768]{1,0:T(1,128)S(1)}, f32[1,768]{1,0:T(1,128)}, u32[]{:S(2)}) copy-start(f32[1,768]{1,0:T(1,128)} %get-tuple-element.66) | copy-start | bytes 9220
  391.2 440.8 %copy-start.8 = (f32[1,768]{1,0:T(1,128)S(1)}, f32[1,768]{1,0:T(1,128)}, u32[]{:S(2)}) copy-start(f32[1,768]{1,0:T(1,128)} %get-tuple-element.67) | copy-start | bytes 9220
  391.8 482.6 %all-gather.15.cloned.1.call-start = ((), (), s32[]{:S(2)}) async-start(), calls=%async_computation.12 | async-start | bytes 5308416 | tf_op jit(solution)/shard_map/all_gather | solution.py:633
  881.4 1.7 copy-start.1
Sparse Core Ops, SparseCore 0:
  11.5 65.6 all-gather.6
  80.7 62.4 all-gather.8
  146.7 62.4 all-gather.10
  212.5 62.4 all-gather.12
  389.9 103.1 reduce-scatter.4
  499.2 106.1 reduce-scatter.6
  610.9 106.0 reduce-scatter.8
  723.4 106.0 reduce-scatter.10
  832.0 40.7 all-gather.14

commit v2 on v1

--- a/solution.py
+++ b/solution.py
@@ -28,6 +28,7 @@
 
 VMEM = pl.BlockSpec(memory_space=pltpu.VMEM)
 SMEM = pl.BlockSpec(memory_space=pltpu.SMEM)
+ANY = pl.BlockSpec(memory_space=pl.ANY)
 LIMIT = 60 * 1024 * 1024
 
 
@@ -80,12 +81,30 @@
     return high, mid, (rest - mid.astype(f32)).astype(bf16)
 
 
-def weight_of(ref, index):
-    return ref[:, index].reshape(D, D)
-
-
-def weight_cols(ref, index, cols):
-    return ref[:, index, :, cols].reshape(D, COLS)
+def weight_copies(core_ref, mine_ref, other_ref, w_s, sem):
+    core = core_ref[0]
+    quarter = D // 4
+    copies = []
+    for h, ref in enumerate((mine_ref, other_ref)):
+        first = 2 * core if h == 0 else 2 * (1 - core)
+        for z in range(4):
+            copies.append(pltpu.make_async_copy(
+                ref.at[z], w_s.at[pl.ds(first, 2), pl.ds(z * quarter, quarter), :],
+                sem.at[4 * h + z]))
+    return copies
+
+
+def put_gradient(keep_ref, send_ref, core_ref, index, cb, value):
+    value = value.astype(bf16).reshape(4, D // 4, COLS)
+    stays = core_ref[0] == index // 2
+
+    @pl.when(stays)
+    def _():
+        keep_ref[:, index % 2, :, cb] = value
+
+    @pl.when(jnp.logical_not(stays))
+    def _():
+        send_ref[:, index % 2, :, cb] = value
 
 
 def put_pairs(dst, cb, value):
@@ -107,17 +126,22 @@
     return lax.broadcasted_iota(jnp.int32, (rows, 128), 1)
 
 
-def self_forward(len_ref, hid_ref, gain1_ref, gain2_ref, lag_ref, u_ref,
+def self_forward(len_ref, core_ref, hid_ref, gain1_ref, gain2_ref, lag_ref, um_ref, uo_ref,
                  n1_ref, q_ref, k_ref, v_ref, lse_ref, mixed_ref, h1_ref, n2_ref,
-                 q_s, k_s, v_s, m_s, bias_s):
+                 q_s, k_s, v_s, m_s, bias_s, w_s, sem):
+    copies = weight_copies(core_ref, um_ref, uo_ref, w_s, sem)
+    for copy in copies:
+        copy.start()
     rows = hid_ref.shape[0]
     count = q_ref.shape[0]
     for rb in row_blocks(rows):
         x = hid_ref[rb, :].astype(f32)
         n1_ref[rb, :] = (x * row_scale(x) * gain1_ref[...]).astype(bf16)
+    for copy in copies:
+        copy.wait()
     for w, dst in enumerate((q_s, k_s, v_s)):
         for cb in col_blocks():
-            put_pairs(dst, cb, rounded(dot(n1_ref[...], weight_cols(u_ref, w, cb))))
+            put_pairs(dst, cb, rounded(dot(n1_ref[...], w_s[w, :, cb])))
         clear_tail(dst, rows)
     starts = starts_of(len_ref)
     row = lax.broadcasted_iota(jnp.int32, (MAX_LEN, MAX_LEN), 0)
@@ -156,28 +180,33 @@
     lax.fori_loop(0, PAIRS, pair, 0)
     join_pairs(mixed_ref, m_s, rows)
     for cb in col_blocks():
-        h1_ref[:, cb] = hid_ref[:, cb].astype(f32) + dot(mixed_ref[...], weight_cols(u_ref, 3, cb))
+        h1_ref[:, cb] = hid_ref[:, cb].astype(f32) + dot(mixed_ref[...], w_s[3, :, cb])
     for rb in row_blocks(rows):
         x = h1_ref[rb, :]
         n2_ref[rb, :] = (x * row_scale(x) * gain2_ref[...]).astype(bf16)
 
 
-def cross_forward(len_ref, n2_ref, h1_ref, gain3_ref, enc_ref, u_ref,
+def cross_forward(len_ref, core_ref, n2_ref, h1_ref, gain3_ref, enc_ref, um_ref, uo_ref,
                   ck_ref, cv_ref, cq_ref, lse_ref, crossed_ref, h2_ref, n3_ref,
-                  q_s, m_s):
+                  q_s, m_s, w_s, sem):
     s = pl.program_id(0)
     rows = n2_ref.shape[0]
     count = pl.num_programs(0)
 
     @pl.when(s == 0)
     def _():
+        copies = weight_copies(core_ref, um_ref, uo_ref, w_s, sem)
+        for copy in copies:
+            copy.start()
+        for copy in copies:
+            copy.wait()
         for cb in col_blocks():
-            put_pairs(q_s, cb, rounded(dot(n2_ref[...], weight_cols(u_ref, 0, cb))))
+            put_pairs(q_s, cb, rounded(dot(n2_ref[...], w_s[0, :, cb])))
         clear_tail(q_s, rows)
 
     for cb in col_blocks():
-        ck_ref[:, cb] = dot(enc_ref[...], weight_cols(u_ref, 1, cb)).astype(bf16)
-        cv_ref[:, cb] = dot(enc_ref[...], weight_cols(u_ref, 2, cb)).astype(bf16)
+        ck_ref[:, cb] = dot(enc_ref[...], w_s[1, :, cb]).astype(bf16)
+        cv_ref[:, cb] = dot(enc_ref[...], w_s[2, :, cb]).astype(bf16)
     start = 0
     for t in range(3):
         start = start + jnp.where(s > t, len_ref[t], 0)
@@ -212,7 +241,7 @@
     def _():
         join_pairs(crossed_ref, m_s, rows)
         for cb in col_blocks():
-            h2_ref[:, cb] = h1_ref[:, cb] + dot(crossed_ref[...], weight_cols(u_ref, 3, cb))
+            h2_ref[:, cb] = h1_ref[:, cb] + dot(crossed_ref[...], w_s[3, :, cb])
         for rb in row_blocks(rows):
             x = h2_ref[rb, :]
             n3_ref[rb, :] = (x * row_scale(x) * gain3_ref[...]).astype(bf16)
@@ -230,7 +259,7 @@
 
 def feed_forward(len_ref, group_ref, step_ref, weight_ref, tags_ref, mask_ref, og_ref, n3_ref,
                  h2_ref, gain3_ref, x_ref, r_ref,
-                 out_ref, gx_ref, gr_ref, g2_ref, gg_ref,
+                 out_ref, gu_ref, g2_ref, gg_ref,
                  scaled_s, out_s, dn_s, act_s, de_s):
     g = pl.program_id(0)
     rows = n3_ref.shape[0]
@@ -267,12 +296,15 @@
         expanded = dot(n3_ref[...], x_ref[:, 0, :, cb].reshape(D, COLS))
         act, slope = gelu_parts(expanded)
         act_s[:, cb] = act.astype(bf16)
-        back = dot_nt(scaled_s[...], r_ref[0, cb, :])
+        back = dot_nt(scaled_s[...], r_ref[0].reshape(D, D)[cb, :])
         de_s[:, cb] = (back * slope).astype(bf16)
     for cb in col_blocks():
-        out_s[:, cb] += dot(act_s[...], r_ref[0, :, cb])
-        gx_ref[:, 0, :, cb] = dot_tn(n3_ref[...], de_s[:, cb]).astype(bf16).reshape(4, D // 4, COLS)
-        gr_ref[0, :, cb] = dot_tn(act_s[...], scaled_s[:, cb]).astype(bf16)
+        out_s[:, cb] += dot(act_s[...], r_ref[0, :, :, cb].reshape(D, COLS))
+        gx = dot_tn(n3_ref[...], de_s[:, cb]).astype(bf16)
+        gr = dot_tn(act_s[...], scaled_s[:, cb]).astype(bf16)
+        gu_ref[g, :, :, cb] = gx.reshape(4, D // 4, COLS)
+        for part in range(4):
+            gu_ref[4 + part, g, :, cb] = gr[part * (D // 4):(part + 1) * (D // 4), :]
     full = x_ref[:, 0].reshape(D, D)
     for cb in col_blocks():
         dn_s[:, cb] += dot_nt(de_s[...], full[cb, :])
@@ -315,20 +347,25 @@
 
 
 def cross_backward(len_ref, g2_ref, crossed_ref, cq_ref, lse_ref, ck_ref, cv_ref, enc_ref, n2_ref,
-                   h1_ref, gain2_ref, u_ref,
-                   ge_ref, gu_ref, g1_ref, gg_ref,
-                   dm_s, dd_s, dq_s, dk_s, dv_s, gk_s, gv_s, b2_s, dml_s, dn_s):
+                   h1_ref, gain2_ref, core_ref, um_ref, uo_ref,
+                   dk_ref, dv_ref, keep_ref, send_ref, g1_ref, gg_ref,
+                   dm_s, dd_s, dq_s, gk_s, gv_s, b2_s, dml_s, dn_s, w_s, sem):
     s = pl.program_id(0)
     rows = g2_ref.shape[0]
 
     @pl.when(s == 0)
     def _():
+        copies = weight_copies(core_ref, um_ref, uo_ref, w_s, sem)
+        for copy in copies:
+            copy.start()
         b2_s[...] = g2_ref[...].astype(bf16)
-        full = weight_of(u_ref, 3)
         for cb in col_blocks():
-            put_pairs(dm_s, cb, rounded(dot_nt(b2_s[...], full[cb, :])))
-            gu_ref[:, 3, :, cb] = dot_tn(crossed_ref[...], b2_s[:, cb]).astype(bf16).reshape(
-                4, D // 4, COLS)
+            put_gradient(keep_ref, send_ref, core_ref, 3, cb,
+                         dot_tn(crossed_ref[...], b2_s[:, cb]))
+        for copy in copies:
+            copy.wait()
+        for cb in col_blocks():
+            put_pairs(dm_s, cb, rounded(dot_nt(b2_s[...], w_s[3, cb, :])))
         clear_tail(dm_s, rows)
         clear_tail(dd_s, rows)
         for hp in range(PAIRS):
@@ -368,34 +405,42 @@
             dq_e = dot_tn(ds, jnp.where(mine_k, k, 0))
             dq, dk, dv = (dq_e, dk_e, dv_e) if e == 0 else (dq + dq_e, dk + dk_e, dv + dv_e)
         dq_s[hp, window, :] = dq
-        dk_s[:, cols] = dk.astype(bf16)
-        dv_s[:, cols] = dv.astype(bf16)
+        dk_ref[:, cols] = dk.astype(bf16)
+        dv_ref[:, cols] = dv.astype(bf16)
         return carry
 
     lax.fori_loop(0, PAIRS, pair, 0)
-    full_k = weight_of(u_ref, 1)
-    full_v = weight_of(u_ref, 2)
-    for cb in col_blocks():
-        gk_s[:, cb] += dot_tn(enc_ref[...], dk_s[:, cb])
-        gv_s[:, cb] += dot_tn(enc_ref[...], dv_s[:, cb])
-        ge_ref[:, cb] = dot_nt(dk_s[...], full_k[cb, :]) + dot_nt(dv_s[...], full_v[cb, :])
+    for cb in col_blocks():
+        gk_s[:, cb] += dot_tn(enc_ref[...], dk_ref[:, cb])
+        gv_s[:, cb] += dot_tn(enc_ref[...], dv_ref[:, cb])
 
     @pl.when(s == pl.num_programs(0) - 1)
     def _():
         join_pairs(dml_s, dq_s, rows)
-        full_q = weight_of(u_ref, 0)
         for cb in col_blocks():
-            gu_ref[:, 0, :, cb] = dot_tn(n2_ref[...], dml_s[:, cb]).astype(bf16).reshape(
-                4, D // 4, COLS)
-            gu_ref[:, 1, :, cb] = gk_s[:, cb].astype(bf16).reshape(4, D // 4, COLS)
-            gu_ref[:, 2, :, cb] = gv_s[:, cb].astype(bf16).reshape(4, D // 4, COLS)
-            dn_s[:, cb] = dot_nt(dml_s[...], full_q[cb, :])
+            put_gradient(keep_ref, send_ref, core_ref, 0, cb, dot_tn(n2_ref[...], dml_s[:, cb]))
+            put_gradient(keep_ref, send_ref, core_ref, 1, cb, gk_s[:, cb])
+            put_gradient(keep_ref, send_ref, core_ref, 2, cb, gv_s[:, cb])
+            dn_s[:, cb] = dot_nt(dml_s[...], w_s[0, cb, :])
         total = jnp.zeros((1, D), f32)
         for rb in row_blocks(rows):
             part, pulled = norm_back(dn_s[rb, :], h1_ref[rb, :], gain2_ref[...])
             g1_ref[rb, :] = g2_ref[rb, :] + part
             total = total + jnp.sum(pulled, axis=0, keepdims=True)
         gg_ref[...] = total
+
+
+def encoded_back(core_ref, dk_ref, dv_ref, um_ref, uo_ref, ge_ref, w_s, sem):
+    @pl.when(pl.program_id(0) == 0)
+    def _():
+        copies = weight_copies(core_ref, um_ref, uo_ref, w_s, sem)
+        for copy in copies:
+            copy.start()
+        for copy in copies:
+            copy.wait()
+
+    for cb in col_blocks():
+        ge_ref[:, cb] = dot_nt(dk_ref[...], w_s[1, cb, :]) + dot_nt(dv_ref[...], w_s[2, cb, :])
 
 
 def diagonal_sums(ref):
@@ -408,18 +453,22 @@
     return jnp.sum(total, axis=0, keepdims=True)
 
 
-def self_backward(len_ref, g1_ref, mixed_ref, q_ref, k_ref, v_ref, lse_ref, n1_ref, hid_ref,
-                  gain1_ref, lag_ref, u_ref,
-                  gh_ref, gu_ref, gg_ref, gl_ref,
-                  dm_s, dd_s, dq_s, dk_s, dv_s, b1_s, low_s, bias_s, acc_s, dn_s):
+def self_backward(len_ref, g1_ref, mixed_ref, q_ref, k_ref, v_ref, lse_ref, n1_ref,
+                  lag_ref, core_ref, um_ref, uo_ref,
+                  dq_ref, dk_ref, dv_ref, keep_ref, send_ref, gl_ref,
+                  dm_s, dd_s, dq_s, dk_s, dv_s, b1_s, bias_s, acc_s, w_s, sem):
+    copies = weight_copies(core_ref, um_ref, uo_ref, w_s, sem)
+    for copy in copies:
+        copy.start()
     rows = g1_ref.shape[0]
     count = q_ref.shape[0]
     b1_s[...] = g1_ref[...].astype(bf16)
-    full = weight_of(u_ref, 3)
-    for cb in col_blocks():
-        put_pairs(dm_s, cb, rounded(dot_nt(b1_s[...], full[cb, :])))
-        gu_ref[:, 3, :, cb] = dot_tn(mixed_ref[...], b1_s[:, cb]).astype(bf16).reshape(
-            4, D // 4, COLS)
+    for cb in col_blocks():
+        put_gradient(keep_ref, send_ref, core_ref, 3, cb, dot_tn(mixed_ref[...], b1_s[:, cb]))
+    for copy in copies:
+        copy.wait()
+    for cb in col_blocks():
+        put_pairs(dm_s, cb, rounded(dot_nt(b1_s[...], w_s[3, cb, :])))
     clear_tail(dm_s, rows)
     clear_tail(dd_s, rows)
     for hp in range(PAIRS):
@@ -470,14 +519,23 @@
         return carry
 
     lax.fori_loop(0, PAIRS, pair, 0)
-    for w, src in enumerate((dq_s, dk_s, dv_s)):
-        join_pairs(low_s, src, rows)
-        full = weight_of(u_ref, w)
+    for w, (src, out) in enumerate(((dq_s, dq_ref), (dk_s, dk_ref), (dv_s, dv_ref))):
+        join_pairs(out, src, rows)
         for cb in col_blocks():
-            gu_ref[:, w, :, cb] = dot_tn(n1_ref[...], low_s[:, cb]).astype(bf16).reshape(
-                4, D // 4, COLS)
-            part = dot_nt(low_s[...], full[cb, :])
-            dn_s[:, cb] = part if w == 0 else dn_s[:, cb] + part
+            put_gradient(keep_ref, send_ref, core_ref, w, cb, dot_tn(n1_ref[...], out[:, cb]))
+
+
+def hidden_back(core_ref, g1_ref, hid_ref, gain1_ref, dq_ref, dk_ref, dv_ref, um_ref, uo_ref,
+                gh_ref, gg_ref, dn_s, w_s, sem):
+    copies = weight_copies(core_ref, um_ref, uo_ref, w_s, sem)
+    for copy in copies:
+        copy.start()
+    for copy in copies:
+        copy.wait()
+    rows = g1_ref.shape[0]
+    for cb in col_blocks():
+        dn_s[:, cb] = (dot_nt(dq_ref[...], w_s[0, cb, :]) + dot_nt(dk_ref[...], w_s[1, cb, :])
+                       + dot_nt(dv_ref[...], w_s[2, cb, :]))
     total = jnp.zeros((1, D), f32)
     for rb in row_blocks(rows):
         part, pulled = norm_back(dn_s[rb, :], hid_ref[rb, :].astype(f32), gain1_ref[...])
@@ -500,12 +558,14 @@
     return jax.ShapeDtypeStruct(dims, kind)
 
 
-def call(kernel, name, outs, ins, scratch, **extra):
+def call(kernel, name, micros, outs, ins, scratch, **extra):
     return pl.pallas_call(
         kernel,
         out_shape=list(outs),
         name=name,
         scratch_shapes=scratch,
+        cost_estimate=pl.CostEstimate(
+            flops=int(micros * 1e9), bytes_accessed=1 << 20, transcendentals=0),
         compiler_params=pltpu.CompilerParams(vmem_limit_bytes=LIMIT),
         **extra,
     )(*ins)
@@ -516,16 +576,85 @@
     return pl.BlockSpec(array_shape, lambda s: zeros)
 
 
-def gather_unit(unit):
-    parts = lax.axis_size("dp")
-    size = D // parts
-    piece = lax.dynamic_slice_in_dim(unit, lax.axis_index("dp") * size, size, 0)
-    return lax.all_gather(piece, ("fsdp", "dp"), axis=0, tiled=True).reshape(4, 4, D // 4, D)
-
-
-def reduce_unit(grads):
-    return lax.psum_scatter(
-        grads.reshape(4 * D, D), ("fsdp", "dp"), scatter_dimension=0, tiled=True)
+class Routes:
+    def __init__(self):
+        self.parts = lax.axis_size("dp")
+        self.shards = lax.axis_size("fsdp")
+        self.dp = lax.axis_index("dp")
+        self.z = lax.axis_index("fsdp")
+        self.core = self.dp & 1
+        bits = list(range(1, self.parts.bit_length() - 1))
+        self.steps = list(zip(bits, bits[::-1]))
+
+    def permute(self, value, partner):
+        pairs = []
+        for dp in range(self.parts):
+            for z in range(self.shards):
+                to_dp, to_z = partner(dp, z)
+                pairs.append((dp * self.shards + z, to_dp * self.shards + to_z))
+        return lax.ppermute(value, ("dp", "fsdp"), pairs)
+
+    def swap_core(self, value):
+        return self.permute(value, lambda dp, z: (dp ^ 1, z))
+
+    def swap(self, value, step):
+        return self.permute(value, lambda dp, z: (dp ^ (1 << step[dp & 1]), z))
+
+    def shift(self, value, by):
+        return self.permute(value, lambda dp, z: (dp, (z + by) % self.shards))
+
+    def bit(self, step):
+        return jnp.where(self.core == 0, (self.dp >> step[0]) & 1, (self.dp >> step[1]) & 1)
+
+    def piece_index(self):
+        index = self.core
+        for step in self.steps:
+            index = 2 * index + self.bit(step)
+        return index
+
+    def gather_shards(self, own):
+        got = [own] + [self.shift(own, by) for by in range(1, self.shards)]
+        return jnp.stack([
+            lax.select_n((self.z - z) % self.shards, *got) for z in range(self.shards)])
+
+    def collect(self, piece):
+        for step in reversed(self.steps):
+            piece = self.join(piece, self.swap(piece, step), step)
+        return piece, self.swap_core(piece)
+
+    def join(self, piece, got, step):
+        return jnp.where(self.bit(step) == 0, jnp.concatenate([piece, got], 1),
+                         jnp.concatenate([got, piece], 1))
+
+    def reduce(self, total, after):
+        for step in self.steps:
+            size = total.shape[2] // 2
+            bit = self.bit(step)
+            send = lax.dynamic_slice_in_dim(total, (1 - bit) * size, size, 2)
+            keep = lax.dynamic_slice_in_dim(total, bit * size, size, 2)
+            got = self.swap(send, step)
+            total = add(keep, tie(got, *after))
+            after = ()
+        return total
+
+    def reduce_shards(self, total):
+        mine = lax.dynamic_index_in_dim(total, self.z, 1, keepdims=False).astype(f32)
+        got = []
+        for by in range(1, self.shards):
+            chunk = lax.dynamic_index_in_dim(
+                total, (self.z + by) % self.shards, 1, keepdims=False)
+            got.append(self.shift(chunk, by))
+        for chunk in got:
+            mine = mine + chunk.astype(f32)
+        return mine.astype(bf16)
+
+
+def add(left, right):
+    return (left.astype(f32) + right.astype(f32)).astype(bf16)
+
+
+def tie(value, *after):
+    return lax.optimization_barrier((value, *after))[0]
 
 
 def per_device(
@@ -537,13 +666,35 @@
     rows = hidden.shape[0]
     count = lengths.shape[0]
     quarter = D // 4
-    u_self = gather_unit(jnp.concatenate([query_weight, key_weight, value_weight, output_weight], 0))
+    routes = Routes()
+    core = routes.core.reshape(1)
+    size = D // routes.parts
+
+    def piece_of(parts, index, extent):
+        return lax.dynamic_slice_in_dim(jnp.concatenate(parts, 0), index * extent, extent, 0)
+
     small = jnp.concatenate([gain_self, gain_cross, gain_ffn, rel_bias.reshape(-1)])
-    small = lax.all_gather(small[None], "fsdp", axis=0, tiled=True).astype(f32)
-    u_cross = gather_unit(jnp.concatenate([cross_query, cross_key, cross_value, cross_output], 0))
-    u_x = gather_unit(
-        jnp.concatenate([expand_weight[:, g * D:(g + 1) * D] for g in range(4)], 0))
-    u_r = gather_unit(reduce_weight)
+    small_row = jnp.pad(small[None], ((0, 15), (0, D - small.shape[0])))
+    own = piece_of([query_weight, key_weight, value_weight, output_weight],
+                   routes.piece_index(), size)
+    first = lax.all_gather(jnp.concatenate([own, small_row], 0)[None], "fsdp", axis=0, tiled=True)
+    u_self = [half.reshape(4, 2, quarter, D) for half in routes.collect(first[:, :size])]
+    small = first[:, size, :small.shape[0]].astype(f32)
+    own = piece_of([cross_query, cross_key, cross_value, cross_output],
+                   routes.piece_index(), size)
+    cross_piece = routes.gather_shards(tie(own, first))
+    for step in routes.steps[:0:-1]:
+        cross_piece = routes.join(cross_piece, routes.swap(cross_piece, step), step)
+    cross_last = routes.swap(cross_piece, routes.steps[0])
+    ratio = routes.parts // 8
+    slot, offset = routes.dp // ratio, (routes.dp % ratio) * (quarter // ratio)
+    own = jnp.where(
+        slot < 4,
+        lax.dynamic_slice(expand_weight, (offset, jnp.minimum(slot, 3) * D), (quarter // ratio, D)),
+        lax.dynamic_slice_in_dim(
+            reduce_weight, jnp.maximum(slot - 4, 0) * quarter + offset, quarter // ratio, 0))
+    u_ffn = lax.all_gather(tie(own, first), ("fsdp", "dp"), axis=0, tiled=True)
+    u_ffn = u_ffn.reshape(4, 8, quarter, D)
 
     gain1 = small[:, 0:quarter].reshape(1, D)
     gain2 = small[:, quarter:2 * quarter].reshape(1, D)
@@ -556,82 +707,113 @@
 
     pad = rows + MAX_LEN
     wide = pltpu.VMEM((PAIRS, pad, 128), f32)
+    low = pltpu.VMEM((rows, D), bf16)
+    flat = pltpu.VMEM((rows, D), f32)
+    square = pltpu.VMEM((2, MAX_LEN, MAX_LEN), f32)
+    weights = [pltpu.VMEM((4, D, D), bf16), pltpu.SemaphoreType.DMA((8,))]
     heads = (count, MAX_LEN, D)
+    halves = (4, 2, quarter, D)
     n1, q, k, v, lse, mixed, h1, n2 = call(
-        self_forward, "self_forward",
+        self_forward, "self_forward", 21,
         (shape((rows, D), bf16), shape(heads, bf16), shape(heads, bf16), shape(heads, bf16),
          shape(heads, f32), shape((rows, D), bf16), shape((rows, D), f32), shape((rows, D), bf16)),
-        (lengths, hidden, gain1, gain2, turned, u_self),
-        [wide, wide, wide, wide, pltpu.VMEM((2, MAX_LEN, MAX_LEN), f32)],
-        in_specs=[SMEM] + [VMEM] * 5, out_specs=[VMEM] * 8)
-
+        (lengths, core, hidden, gain1, gain2, turned, *u_self),
+        [wide, wide, wide, wide, square] + weights,
+        in_specs=[SMEM] * 2 + [VMEM] * 4 + [ANY] * 2, out_specs=[VMEM] * 8)
+
+    cross_piece = routes.join(cross_piece, tie(cross_last, n2), routes.steps[0])
+    u_cross = [half.reshape(4, 2, quarter, D)
+               for half in (cross_piece, routes.swap_core(cross_piece))]
     enc_block = pl.BlockSpec((ENC_LEN, D), lambda s: (s, 0))
     seq_block = pl.BlockSpec((1, MAX_LEN, D), lambda s: (s, 0, 0))
-    unit = whole((4, 4, quarter, D))
     full = whole((rows, D))
     line = whole((1, D))
     ck, cv, cq, cross_lse, crossed, h2, n3 = call(
-        cross_forward, "cross_forward",
+        cross_forward, "cross_forward", 34,
         (shape(encoded.shape, bf16), shape(encoded.shape, bf16), shape(heads, bf16),
          shape(heads, f32), shape((rows, D), bf16), shape((rows, D), f32), shape((rows, D), bf16)),
-        (lengths, n2, h1, gain3, encoded, u_cross),
-        [wide, wide],
+        (lengths, core, n2, h1, gain3, encoded, *u_cross),
+        [wide, wide] + weights,
         grid=(count,),
-        in_specs=[SMEM, full, full, line, enc_block, unit],
+        in_specs=[SMEM] * 2 + [full, full, line, enc_block, ANY, ANY],
         out_specs=[enc_block, enc_block, seq_block, seq_block, full, full, full])
 
     column = whole((rows, 1))
     x_block = pl.BlockSpec((4, 1, quarter, D), lambda g: (0, g, 0, 0))
-    r_block = pl.BlockSpec((1, D, D), lambda g: (g, 0, 0))
-    low = pltpu.VMEM((rows, D), bf16)
-    flat = pltpu.VMEM((rows, D), f32)
-    layer_output, grad_x, grad_r, g2, gg3 = call(
-        feed_forward, "feed_forward",
-        (shape((rows, D), bf16), shape((4, 4, quarter, D), bf16), shape((4, D, D), bf16),
+    r_block = pl.BlockSpec((1, 4, quarter, D), lambda g: (g, 1, 0, 0))
+    layer_output, grad_ffn, g2, gg3 = call(
+        feed_forward, "feed_forward", 32,
+        (shape((rows, D), bf16), shape((8, 4, quarter, D), bf16),
          shape((rows, D), f32), shape((1, D), f32)),
         (lengths, group_ids, group_steps, group_weights, id_tags[:, None], loss_mask[:, None],
-         out_grad, n3, h2, gain3, u_x, u_r.reshape(4, D, D)),
+         out_grad, n3, h2, gain3, u_ffn, u_ffn),
         [low, flat, flat, low, low],
         grid=(4,),
         in_specs=[SMEM] * 4 + [column, column, full, full, full, line, x_block, r_block],
-        out_specs=[full, x_block, r_block, full, line])
-    piece_x = reduce_unit(grad_x)
-    piece_r = reduce_unit(grad_r)
-
-    grad_encoded, grad_cross, g1, gg2 = call(
-        cross_backward, "cross_backward",
-        (shape(encoded.shape, f32), shape((4, 4, quarter, D), bf16), shape((rows, D), f32),
-         shape((1, D), f32)),
-        (lengths, g2, crossed, cq, cross_lse, ck, cv, encoded, n2, h1, gain2, u_cross),
-        [wide, wide, wide, pltpu.VMEM((ENC_LEN, D), bf16), pltpu.VMEM((ENC_LEN, D), bf16),
-         pltpu.VMEM((D, D), f32), pltpu.VMEM((D, D), f32), low, low, flat],
+        out_specs=[full, whole((8, 4, quarter, D)), full, line])
+    if routes.parts > 8:
+        grad_ffn = grad_ffn.reshape(8, 4, routes.parts // 8, -1, D).swapaxes(1, 2)
+    ffn_piece = lax.psum_scatter(
+        grad_ffn.reshape(-1, D), "dp", scatter_dimension=0, tiled=True)
+
+    dck, dcv, keep, send, g1, gg2 = call(
+        cross_backward, "cross_backward", 42,
+        (shape(encoded.shape, bf16), shape(encoded.shape, bf16), shape(halves, bf16),
+         shape(halves, bf16), shape((rows, D), f32), shape((1, D), f32)),
+        (lengths, g2, crossed, cq, cross_lse, ck, cv, encoded, n2, h1, gain2, core, *u_cross),
+        [wide, wide, wide, pltpu.VMEM((D, D), f32), pltpu.VMEM((D, D), f32), low, low, flat]
+        + weights,
         grid=(count,),
         in_specs=[SMEM, full, full, seq_block, seq_block, enc_block, enc_block, enc_block, full,
-                  full, line, unit],
-        out_specs=[enc_block, unit, full, line])
-    piece_cross = reduce_unit(grad_cross)
-
-    grad_hidden, grad_self, gg1, grad_lag = call(
-        self_backward, "self_backward",
-        (shape((rows, D), f32), shape((4, 4, quarter, D), bf16), shape((1, D), f32),
-         shape((HEADS, MAX_LEN), f32)),
-        (lengths, g1, mixed, q, k, v, lse, n1, hidden, gain1, by_lag, u_self),
-        [wide, wide, wide, wide, wide, low, low,
-         pltpu.VMEM((2, MAX_LEN, MAX_LEN), f32), pltpu.VMEM((2, MAX_LEN, MAX_LEN), f32), flat],
-        in_specs=[SMEM] + [VMEM] * 11, out_specs=[VMEM] * 4)
-    piece_self = reduce_unit(grad_self)
-
+                  full, line, SMEM, ANY, ANY],
+        out_specs=[enc_block, enc_block, whole(halves), whole(halves), full, line])
+    cross_keep = keep
+    cross_got = routes.swap_core(send)
+
+    dq, dk, dv, keep, send, grad_lag = call(
+        self_backward, "self_backward", 28,
+        (shape((rows, D), bf16), shape((rows, D), bf16), shape((rows, D), bf16),
+         shape(halves, bf16), shape(halves, bf16), shape((HEADS, MAX_LEN), f32)),
+        (lengths, g1, mixed, q, k, v, lse, n1, by_lag, core, *u_self),
+        [wide, wide, wide, wide, wide, low, square, square] + weights,
+        in_specs=[SMEM] + [VMEM] * 8 + [SMEM, ANY, ANY], out_specs=[VMEM] * 6)
+    self_got = routes.swap_core(send)
+
+    grad_hidden, gg1 = call(
+        hidden_back, "hidden_back", 8,
+        (shape((rows, D), f32), shape((1, D), f32)),
+        (core, g1, hidden, gain1, dq, dk, dv, *u_self),
+        [flat] + weights,
+        in_specs=[SMEM] + [VMEM] * 6 + [ANY] * 2, out_specs=[VMEM] * 2)
+    total = jnp.stack([add(keep, tie(self_got, grad_hidden)), add(cross_keep, cross_got)])
+    total = total.reshape(2, 4, D // 2, D)
+
+    (grad_encoded,) = call(
+        encoded_back, "encoded_back", 10,
+        (shape(encoded.shape, f32),),
+        (core, tie(dck, total), dcv, *u_cross),
+        weights,
+        grid=(count,),
+        in_specs=[SMEM, enc_block, enc_block, ANY, ANY], out_specs=[enc_block])
     grad_rel = lax.dot_general(
         grad_lag, jnp.asarray(table), (((1,), (1,)), ((), ())), precision=lax.Precision.HIGHEST)
     small_grads = jnp.concatenate(
         [gg1.reshape(4, quarter), gg2.reshape(4, quarter), gg3.reshape(4, quarter),
          grad_rel.reshape(4, -1)], axis=1)
-    small_total = lax.psum(small_grads, ("dp", "fsdp"))
-    small_mine = lax.dynamic_slice_in_dim(small_total, lax.axis_index("fsdp"), 1, 0)[0]
-
-    pieces = jnp.stack([piece_self, piece_cross, piece_x, piece_r])
-    shards = lax.all_gather(pieces, "dp", axis=1, tiled=True).astype(f32)
-    blocks = shards.reshape(4, 4, quarter, D)
+    extent = ffn_piece.shape[0] // 4
+    small_rows = jnp.pad(small_grads.astype(bf16)[:, None, :],
+                         ((0, 0), (0, 15), (0, D - small_grads.shape[1])))
+    ffn_piece = jnp.concatenate(
+        [tie(ffn_piece, total).reshape(4, extent, D), small_rows], axis=1)
+    ffn_piece = lax.psum_scatter(ffn_piece.reshape(-1, D), "fsdp", scatter_dimension=0, tiled=True)
+    ffn_shard = lax.all_gather(ffn_piece[None], "dp", axis=0, tiled=True).astype(f32)
+    small_mine = jnp.sum(ffn_shard[:, extent], axis=0)
+    ffn = ffn_shard[:, :extent].reshape(2 * D, D)
+
+    piece = routes.reduce_shards(routes.reduce(total, (grad_encoded,)))
+    mine, other = routes.collect(piece)
+    low_half = jnp.where(routes.core == 0, mine, other).astype(f32).reshape(2, 2, quarter, D)
+    high_half = jnp.where(routes.core == 0, other, mine).astype(f32).reshape(2, 2, quarter, D)
     return (
         layer_output,
         grad_hidden,
@@ -639,17 +821,17 @@
         small_mine[0:quarter],
         small_mine[quarter:2 * quarter],
         small_mine[2 * quarter:3 * quarter],
-        small_mine[3 * quarter:].reshape(HEADS // 4, BUCKETS),
-        blocks[0, 0],
-        blocks[0, 1],
-        blocks[0, 2],
-        blocks[0, 3],
-        blocks[1, 0],
-        blocks[1, 1],
-        blocks[1, 2],
-        blocks[1, 3],
-        jnp.concatenate([blocks[2, g] for g in range(4)], axis=1),
-        shards[3],
+        small_mine[3 * quarter:small_grads.shape[1]].reshape(HEADS // 4, BUCKETS),
+        low_half[0, 0],
+        low_half[0, 1],
+        high_half[0, 0],
+        high_half[0, 1],
+        low_half[1, 0],
+        low_half[1, 1],
+        high_half[1, 0],
+        high_half[1, 1],
+        jnp.concatenate([ffn[g * quarter:(g + 1) * quarter] for g in range(4)], axis=1),
+        ffn[D:],
     )
 
 

time: 901 us -> 433 us (0.48)
  waiting for transfers between devices: 631 us -> 128 us
  blocking collectives: 48.2 us -> 14.4 us
  starting transfers between devices: 0.36 us -> 28.3 us
  Pallas kernels: 170 us -> 197 us
  other arithmetic: 11.7 us -> 27.7 us
    reduce_scatter x4 -> x2, waiting for transfers between devices: 438 us -> 0.02 us  [the longest x1 0.02 us: per_device(): lax.psum_scatter(grad_ffn.reshape(-1, D), 'dp', scatter_dimension=0, tile...]
    all_gather x5 -> x2, waiting for transfers between devices: 192 us -> 0.02 us  [the longest x1 0.02 us: per_device(): u_ffn = lax.all_gather(tie(own, first), ('fsdp', 'dp'), axis=0, tiled=True)]
    ppermute x0 -> x19, waiting for transfers between devices: none -> 128 us  [permute(): return lax.ppermute(value, ('dp', 'fsdp'), pairs)]
    psum x1 -> x0, blocking collectives: 40.9 us -> none  [per_device(): small_total = lax.psum(small_grads, ('dp', 'fsdp'))]
    ppermute x0 -> x19, starting transfers between devices: none -> 28.1 us  [permute(): return lax.ppermute(value, ('dp', 'fsdp'), pairs)]
    pallas_call x5 -> x7, Pallas kernels: 170 us -> 197 us  [call(): pl.pallas_call(kernel, out_shape=list(outs), name=name, scratch_shapes=sc...]
    all_gather x0 -> x1, blocking collectives: none -> 14.4 us  [per_device(): lax.all_gather(jnp.concatenate([own, small_row], 0)[None], 'fsdp', axis=0...]
  transfers between devices with their start and end apart: 9 -> 23, of which waited for: 8 -> 15; matrix products, arithmetic and copies ran while one was open for 1% -> 7% of each run, Pallas kernels for 6% -> 38%
where the time goes in v2:
time: 433 us; the launch traced here: 429 us
  Pallas kernels  197 us (45%)
  waiting for transfers between devices  128 us (30%)
  starting transfers between devices  28.3 us (7%)
  other arithmetic  27.7 us (6%)
  local copies, waits for them, and re-layouts  16.3 us (4%)
  between operations  14.5 us (3%)
  blocking collectives  14.4 us (3%)
    pallas_call x7, Pallas kernels, call(): pl.pallas_call(kernel, out_shape=list(outs), name=name, scratch_shapes=sc...  197 us
    ppermute x19, waiting for transfers between devices, permute(): return lax.ppermute(value, ('dp', 'fsdp'), pairs)  128 us
    ppermute x19, starting transfers between devices, permute(): return lax.ppermute(value, ('dp', 'fsdp'), pairs)  28.1 us
    all_gather x1, blocking collectives, per_device(): lax.all_gather(jnp.concatenate([own, small_row], 0)[None], 'fsdp', axis=0...  14.4 us
    convert_element_type x4, other arithmetic, add(): return (left.astype(f32) + right.astype(f32)).astype(bf16)  9.42 us
  transfers between devices with their start and end apart: 23, of which 15 were waited for; matrix products, arithmetic and copies ran while one was open for 7% of the time, Pallas kernels for 38%

profile of v2, /device:TPU:9, one launch (start us, length us, event | category | flops | bytes accessed | tf_op | source)
XLA Modules:
  0.0 428.5 jit_solution(5483079332042755899)
XLA Ops:
  9.9 14.4 %all-gather = bf16[448,768]{1,0:T(8,128)(2,1)S(1)} all-gather(bf16[112,768]{1,0:T(8,128)(2,1)S(1)} %fusion.8), channel_id=2, replica_groups=mesh['dp'=8,'fsdp'=4] {'fsdp'}, dimensions={0}, use_global_device_ids=true | all-gather | bytes 860160 | tf_op jit(solution)/shard_map/all_gather | solution.py:680
  27.5 7.8 %collective-permute-done = bf16[4,96,768]{2,1,0:T(8,128)(2,1)S(1)} collective-permute-done((bf16[4,96,768]{2,1,0:T(8,128)(2,1)S(1)}, bf16[4,96,768]{2,1,0:T(8,128)(2,1)S(1)}, u32[]{:S(2)}, u32[]{:S(2)}) %collective-permute-start) | collective-permute-done | bytes 589856 | tf_op jit(solution)/shard_map/ppermute | solution.py:595
  37.1 17.1 %collective-permute-done.1 = bf16[4,192,768]{2,1,0:T(8,128)(2,1)S(1)} collective-permute-done((bf16[4,192,768]{2,1,0:T(8,128)(2,1)S(1)}, bf16[4,192,768]{2,1,0:T(8,128)(2,1)S(1)}, u32[]{:S(2)}, u32[]{:S(2)}) %collective-permute-start.1) | collective-permute-done | bytes 1179680 | tf_op jit(solution)/shard_map/ppermute | solution.py:595
  55.9 3.2 collective-permute-start.2
  60.4 2.9 collective-permute-start.4
  63.8 5.5 %collective-permute-done.3 = bf16[96,768]{1,0:T(8,128)(2,1)S(1)} collective-permute-done((bf16[96,768]{1,0:T(8,128)(2,1)S(1)}, bf16[96,768]{1,0:T(8,128)(2,1)S(1)}, u32[]{:S(2)}, u32[]{:S(2)}) %collective-permute-start.3) | collective-permute-done | bytes 147488 | tf_op jit(solution)/shard_map/ppermute | solution.py:595
  69.4 13.9 %collective-permute-done.4 = bf16[96,768]{1,0:T(8,128)(2,1)S(1)} collective-permute-done((bf16[96,768]{1,0:T(8,128)(2,1)S(1)}, bf16[96,768]{1,0:T(8,128)(2,1)S(1)}, u32[]{:S(2)}, u32[]{:S(2)}) %collective-permute-start.4) | collective-permute-done | bytes 147488 | tf_op jit(solution)/shard_map/ppermute | solution.py:595
  83.3 2.3 collective-permute-done.5
  89.3 11.0 %collective-permute-done.6 = bf16[4,96,768]{2,1,0:T(8,128)(2,1)S(1)} collective-permute-done((bf16[4,96,768]{2,1,0:T(8,128)(2,1)S(1)}, bf16[4,96,768]{2,1,0:T(8,128)(2,1)S(1)}, u32[]{:S(2)}, u32[]{:S(2)}) %collective-permute-start.6) | collective-permute-done | bytes 589856 | tf_op jit(solution)/shard_map/ppermute | solution.py:595
  101.9 22.3 %self_forward.1 = (bf16[640,768]{1,0:T(8,128)(2,1)}, bf16[4,256,768]{2,1,0:T(8,128)(2,1)}, bf16[4,256,768]{2,1,0:T(8,128)(2,1)}, bf16[4,256,768]{2,1,0:T(8,128)(...) custom-call(s32[4]{0:T(128)} %len_ref.9, ...), custom_call_target="tpu_custom_call" | custom-call | flops 20999999488 | bytes 1048576 | tf_op jit(solution)/shard_map/self_forward/pallas_call | solution.py:562
  128.5 2.4 collective-permute-start.8
  135.2 35.3 %cross_forward.1 = (bf16[2048,768]{1,0:T(8,128)(2,1)}, bf16[2048,768]{1,0:T(8,128)(2,1)}, bf16[4,256,768]{2,1,0:T(8,128)(2,1)}, f32[4,256,768]{2,1,0:T(8,128)}, ...) custom-call(s32[4]{0:T(128)} %len_ref.9, s32[1]{0:T(128)} %bitcast.core_ref, ...), custom_call_target="tpu_custom_call" | custom-call | flops 33999998976 | bytes 1048576 | tf_op jit(solution)/shard_map/cross_forward/pallas_call | solution.py:562
  170.5 34.6 %feed_forward.1 = (bf16[640,768]{1,0:T(8,128)(2,1)}, bf16[8,4,192,768]{3,2,1,0:T(8,128)(2,1)}, f32[640,768]{1,0:T(8,128)}, f32[1,768]{1,0:T(1,128)}) custom-call(s32[4]{0:T(128)} %len_ref.9, s32[4]{0:T(128)} %group_ref.1, s32[3]{0:T(128)} %step_ref.1, s32[3]{0:T(128)} %weight_ref.1, s32[640,1]{1,0:T(8,128)} %broadcast_in_dim.21.tags_ref, ...), custom_call_target="tpu_custom_call" | custom-call | flops 32000000000 | bytes 1048576 | tf_op jit(solution)/shard_map/feed_forward/pallas_call | solution.py:562
  206.6 49.1 %cross_backward.1 = (bf16[2048,768]{1,0:T(8,128)(2,1)}, bf16[2048,768]{1,0:T(8,128)(2,1)}, bf16[4,2,192,768]{3,2,1,0:T(8,128)(2,1)}, bf16[4,2,192,768]{3,2,1,0:T...) custom-call(s32[4]{0:T(128)} %len_ref.9, f32[640,768]{1,0:T(8,128)} %get-tuple-element.65.g2_ref, ...), custom_call_target="tpu_custom_call" | custom-call | flops 41999998976 | bytes 1048576 | tf_op jit(solution)/shard_map/cross_backward/pallas_call | solution.py:562
  255.7 35.3 %self_backward.1 = (bf16[640,768]{1,0:T(8,128)(2,1)}, bf16[640,768]{1,0:T(8,128)(2,1)}, bf16[640,768]{1,0:T(8,128)(2,1)}, bf16[4,2,192,768]{3,2,1,0:T(8,128)(2,1...) custom-call(s32[4]{0:T(128)} %len_ref.9, f32[640,768]{1,0:T(8,128)} %get-tuple-element.71.g1_ref, ...), custom_call_target="tpu_custom_call" | custom-call | flops 28000000000 | bytes 1048576 | tf_op jit(solution)/shard_map/self_backward/pallas_call | solution.py:562
  291.8 9.3 %hidden_back.1 = (f32[640,768]{1,0:T(8,128)}, f32[1,768]{1,0:T(1,128)}) custom-call(s32[1]{0:T(128)} %bitcast.core_ref, f32[640,768]{1,0:T(8,128)} %get-tuple-element.71.g1_ref, bf16[640,768]{1,0:T(8,128)(2,1)} %hid_ref.3, f32[1,768]{1,0:T(1,128)} %reshape.185.gain1_ref, bf16[640,768]{1,0:T(8,128)(2,1)} %get-tuple-element.78.dq_ref, ...), custom_call_target="tpu_custom_call" | custom-call | flops 8000000000 | bytes 1048576 | tf_op jit(solution)/shard_map/hidden_back/pallas_call | solution.py:562
  302.6 3.1 add_convert_fusion.2
  305.7 2.2 add_convert_fusion.1
  310.0 3.4 collective-permute-start.11
  314.1 2.4 fusion.3
  316.6 11.4 %encoded_back.1 = f32[2048,768]{1,0:T(8,128)} custom-call(s32[1]{0:T(128)} %bitcast.core_ref, bf16[2048,768]{1,0:T(8,128)(2,1)} %get-tuple-element.88.dk_ref, bf16[2048,768]{1,0:T(8,128)(2,1)} %get-tuple-element.89.dv_ref, bf16[4,2,192,768]{3,2,1,0:T(8,128)(2,1)} %bitcast.83, bf16[4,2,192,768]{3,2,1,0:T(8,128)(2,1)} %bitcast.9.uo_ref), custom_call_target="tpu_custom_call" | custom-call | flops 10000000000 | bytes 1048576 | tf_op jit(solution)/shard_map/encoded_back/pallas_call | solution.py:562
  328.0 12.2 %collective-permute-done.11 = bf16[2,4,192,768]{3,2,1,0:T(8,128)(2,1)} collective-permute-done((bf16[2,4,192,768]{3,2,1,0:T(8,128)(2,1)}, bf16[2,4,192,768]{3,2,1,0:T(8,128)(2,1)}, u32[]{:S(2)}, u32[]{:S(2)}) %collective-permute-start.11) | collective-permute-done | bytes 2359328 | tf_op jit(solution)/shard_map/ppermute | solution.py:595
  340.2 2.6 add_convert_fusion
  345.4 17.7 %collective-permute-done.12 = bf16[2,4,96,768]{3,2,1,0:T(8,128)(2,1)S(1)} collective-permute-done((bf16[2,4,96,768]{3,2,1,0:T(8,128)(2,1)S(1)}, bf16[2,4,96,768]{3,2,1,0:T(8,128)(2,1)S(1)}, u32[]{:S(2)}, u32[]{:S(2)}) %collective-permute-start.12) | collective-permute-done | bytes 1179680 | tf_op jit(solution)/shard_map/ppermute | solution.py:595
  366.3 5.5 %collective-permute-done.13 = bf16[2,96,768]{2,1,0:T(8,128)(2,1)S(1)} collective-permute-done((bf16[2,96,768]{2,1,0:T(8,128)(2,1)S(1)}, bf16[2,96,768]{2,1,0:T(8,128)(2,1)S(1)}, u32[]{:S(2)}, u32[]{:S(2)}) %collective-permute-start.13) | collective-permute-done | bytes 294944 | tf_op jit(solution)/shard_map/ppermute | solution.py:595
  371.7 16.9 %collective-permute-done.14 = bf16[2,96,768]{2,1,0:T(8,128)(2,1)S(1)} collective-permute-done((bf16[2,96,768]{2,1,0:T(8,128)(2,1)S(1)}, bf16[2,96,768]{2,1,0:T(8,128)(2,1)S(1)}, u32[]{:S(2)}, u32[]{:S(2)}) %collective-permute-start.14) | collective-permute-done | bytes 294944 | tf_op jit(solution)/shard_map/ppermute | solution.py:595
  389.7 5.1 %collective-permute-done.16 = bf16[2,96,768]{2,1,0:T(8,128)(2,1)S(1)} collective-permute-done((bf16[2,96,768]{2,1,0:T(8,128)(2,1)S(1)}, bf16[2,96,768]{2,1,0:T(8,128)(2,1)S(1)}, u32[]{:S(2)}, u32[]{:S(2)}) %collective-permute-start.16) | collective-permute-done | bytes 294944 | tf_op jit(solution)/shard_map/ppermute | solution.py:595
  396.2 7.8 %collective-permute-done.17 = bf16[2,192,768]{2,1,0:T(8,128)(2,1)S(1)} collective-permute-done((bf16[2,192,768]{2,1,0:T(8,128)(2,1)S(1)}, bf16[2,192,768]{2,1,0:T(8,128)(2,1)S(1)}, u32[]{:S(2)}, u32[]{:S(2)}) %collective-permute-start.17) | collective-permute-done | bytes 589856 | tf_op jit(solution)/shard_map/ppermute | solution.py:595
  404.5 4.1 collective-permute-start.18
  408.6 2.5 collective-permute-done.18
  411.6 2.2 slice_bitcast_fusion.4
  413.8 2.2 convert.25
  (123 shorter events, 46.4 us)
Async XLA Ops:
  7.2 163.3 %all-gather.5.cloned.1.call-start = ((), (), s32[]{:S(2)}) async-start(), calls=%async_computation.2 | async-start | bytes 9732096 | tf_op jit(solution)/shard_map/all_gather | solution.py:696
  26.1 287.9 %reduce-scatter.3.cloned.1.call-start = ((), (), s32[]{:S(2)}) async-start(), calls=%async_computation.3 | async-start | bytes 10616832 | tf_op jit(solution)/shard_map/reduce_scatter | solution.py:756
  26.2 9.1 %collective-permute-start = (bf16[4,96,768]{2,1,0:T(8,128)(2,1)S(1)}, bf16[4,96,768]{2,1,0:T(8,128)(2,1)S(1)}, u32[]{:S(2)}, u32[]{:S(2)}) collective-permute-start(bf16[4,96,768]{2,1,0:T(8,128)(2,1)S(1)} %slice.134), channel_id=1, source_target_pairs={{0,16},{1,17},{2,18},{3,19},{4,12},{5,13},{6,14},{7,15},{8,24},{9,... | collective-permute-start | bytes 1769480 | tf_op jit(solution)/shard_map/ppermute | solution.py:595
  35.8 18.4 %collective-permute-start.1 = (bf16[4,192,768]{2,1,0:T(8,128)(2,1)S(1)}, bf16[4,192,768]{2,1,0:T(8,128)(2,1)S(1)}, u32[]{:S(2)}, u32[]{:S(2)}) collective-permute-start(bf16[4,192,768]{2,1,0:T(8,128)(2,1)S(1)} %maximum_select_fusion.2), channel_id=1, source_target_pairs={{0,8},{1,9},{2,10},{3,11},{4,20},{5,21},{6,22},{7,23},{8,0},{9,1},... | collective-permute-start | bytes 3538952 | tf_op jit(solution)/shard_map/ppermute | solution.py:595
  37.1 22.1 %copy-start.7 = (bf16[192,768]{1,0:T(8,128)(2,1)S(1)}, bf16[192,768]{1,0:T(8,128)(2,1)}, u32[]{:S(2)}) copy-start(bf16[192,768]{1,0:T(8,128)(2,1)} %param.45) | copy-start | bytes 884740
  37.1 22.1 %copy-start.8 = (bf16[192,768]{1,0:T(8,128)(2,1)S(1)}, bf16[192,768]{1,0:T(8,128)(2,1)}, u32[]{:S(2)}) copy-start(bf16[192,768]{1,0:T(8,128)(2,1)} %param.44) | copy-start | bytes 884740
  37.1 22.1 %copy-start.9 = (bf16[192,768]{1,0:T(8,128)(2,1)S(1)}, bf16[192,768]{1,0:T(8,128)(2,1)}, u32[]{:S(2)}) copy-start(bf16[192,768]{1,0:T(8,128)(2,1)} %param.43) | copy-start | bytes 884740
  37.1 22.1 %copy-start.10 = (bf16[192,768]{1,0:T(8,128)(2,1)S(1)}, bf16[192,768]{1,0:T(8,128)(2,1)}, u32[]{:S(2)}) copy-start(bf16[192,768]{1,0:T(8,128)(2,1)} %param.42) | copy-start | bytes 884740
  55.9 32.7 %copy-start.12 = (f32[32,256]{1,0:T(8,128)S(1)}, f32[32,256]{1,0:T(8,128)}, u32[]{:S(2)}) copy-start(f32[32,256]{1,0:T(8,128)} %constant.107.clone) | copy-start | bytes 98308
  55.9 46.0 %collective-permute-start.2 = (bf16[4,384,768]{2,1,0:T(8,128)(2,1)}, bf16[4,384,768]{2,1,0:T(8,128)(2,1)}, u32[]{:S(2)}, u32[]{:S(2)}) collective-permute-start(bf16[4,384,768]{2,1,0:T(8,128)(2,1)} %maximum_select_fusion), channel_id=1, source_target_pairs={{0,4},{1,5},{2,6},{3,7},{4,0},{5,1},{6,2},{7,3},{8,12},{9,13},{10,... | collective-permute-start | bytes 7077896 | tf_op jit(solution)/shard_map/ppermute | solution.py:595
  59.5 9.9 %collective-permute-start.3 = (bf16[96,768]{1,0:T(8,128)(2,1)S(1)}, bf16[96,768]{1,0:T(8,128)(2,1)S(1)}, u32[]{:S(2)}, u32[]{:S(2)}) collective-permute-start(bf16[96,768]{1,0:T(8,128)(2,1)S(1)} %fusion.11), channel_id=1, source_target_pairs={{0,1},{1,2},{2,3},{3,0},{4,5},{5,6},{6,7},{7,4},{8,9},{9,10},{10,1... | collective-permute-start | bytes 442376 | tf_op jit(solution)/shard_map/ppermute | solution.py:595
  60.4 22.9 %collective-permute-start.4 = (bf16[96,768]{1,0:T(8,128)(2,1)S(1)}, bf16[96,768]{1,0:T(8,128)(2,1)S(1)}, u32[]{:S(2)}, u32[]{:S(2)}) collective-permute-start(bf16[96,768]{1,0:T(8,128)(2,1)S(1)} %fusion.11), channel_id=1, source_target_pairs={{0,2},{1,3},{2,0},{3,1},{4,6},{5,7},{6,4},{7,5},{8,10},{9,11},{10,... | collective-permute-start | bytes 442376 | tf_op jit(solution)/shard_map/ppermute | solution.py:595
  63.3 22.3 %collective-permute-start.5 = (bf16[96,768]{1,0:T(8,128)(2,1)S(1)}, bf16[96,768]{1,0:T(8,128)(2,1)S(1)}, u32[]{:S(2)}, u32[]{:S(2)}) collective-permute-start(bf16[96,768]{1,0:T(8,128)(2,1)S(1)} %fusion.11), channel_id=1, source_target_pairs={{0,3},{1,0},{2,1},{3,2},{4,7},{5,4},{6,5},{7,6},{8,11},{9,8},{10,9... | collective-permute-start | bytes 442376 | tf_op jit(solution)/shard_map/ppermute | solution.py:595
  85.7 14.6 %collective-permute-start.6 = (bf16[4,96,768]{2,1,0:T(8,128)(2,1)S(1)}, bf16[4,96,768]{2,1,0:T(8,128)(2,1)S(1)}, u32[]{:S(2)}, u32[]{:S(2)}) collective-permute-start(bf16[4,96,768]{2,1,0:T(8,128)(2,1)S(1)} %pad_maximum_fusion.2), channel_id=1, source_target_pairs={{0,16},{1,17},{2,18},{3,19},{4,12},{5,13},{6,14},{7,15},{8,24},{9,... | collective-permute-start | bytes 1769480 | tf_op jit(solution)/shard_map/ppermute | solution.py:595
  100.6 24.7 %collective-permute-start.7 = (bf16[4,192,768]{2,1,0:T(8,128)(2,1)S(1)}, bf16[4,192,768]{2,1,0:T(8,128)(2,1)S(1)}, u32[]{:S(2)}, u32[]{:S(2)}) collective-permute-start(bf16[4,192,768]{2,1,0:T(8,128)(2,1)S(1)} %maximum_select_fusion.3), channel_id=1, source_target_pairs={{0,8},{1,9},{2,10},{3,11},{4,20},{5,21},{6,22},{7,23},{8,0},{9,1},... | collective-permute-start | bytes 3538952 | tf_op jit(solution)/shard_map/ppermute | solution.py:595
  126.4 6.1 %copy-start.15 = (s32[640]{0:T(1024)S(1)}, s32[640]{0:T(1024)}, u32[]{:S(2)}) copy-start(s32[640]{0:T(1024)} %param.31) | copy-start | bytes 7684
  128.5 6.7 %copy-start.5 = (bf16[4,384,768]{2,1,0:T(8,128)(2,1)}, bf16[4,384,768]{2,1,0:T(8,128)(2,1)S(1)}, u32[]{:S(2)}) copy-start(bf16[4,384,768]{2,1,0:T(8,128)(2,1)S(1)} %maximum_select_fusion.1) | copy-start | bytes 7077892
  128.5 6.7 %collective-permute-start.8 = (bf16[4,384,768]{2,1,0:T(8,128)(2,1)S(1)}, bf16[4,384,768]{2,1,0:T(8,128)(2,1)}, u32[]{:S(2)}, u32[]{:S(2)}) collective-permute-start(bf16[4,384,768]{2,1,0:T(8,128)(2,1)S(1)} %maximum_select_fusion.1), channel_id=1, source_target_pairs={{0,4},{1,5},{2,6},{3,7},{4,0},{5,1},{6,2},{7,3},{8,12},{9,13},{10,... | collective-permute-start | bytes 7077896 | tf_op jit(solution)/shard_map/ppermute | solution.py:595
  205.1 140.2 %reduce-scatter.5.cloned.1.call-start = ((), (), s32[]{:S(2)}) async-start(), calls=%async_computation.4 | async-start | bytes 1597440 | tf_op jit(solution)/shard_map/reduce_scatter | solution.py:808
  291.0 10.1 %collective-permute-start.9 = (bf16[4,2,192,768]{3,2,1,0:T(8,128)(2,1)}, bf16[4,2,192,768]{3,2,1,0:T(8,128)(2,1)S(1)}, u32[]{:S(2)}, u32[]{:S(2)}) collective-permute-start(bf16[4,2,192,768]{3,2,1,0:T(8,128)(2,1)} %get-tuple-element.84), channel_id=1, source_target_pairs={{0,4},{1,5},{2,6},{3,7},{4,0},{5,1},{6,2},{7,3},{8,12},{9,13},{10,... | collective-permute-start | bytes 7077896 | tf_op jit(solution)/shard_map/ppermute | solution.py:595
  291.8 13.9 %collective-permute-start.10 = (bf16[4,2,192,768]{3,2,1,0:T(8,128)(2,1)}, bf16[4,2,192,768]{3,2,1,0:T(8,128)(2,1)}, u32[]{:S(2)}, u32[]{:S(2)}) collective-permute-start(bf16[4,2,192,768]{3,2,1,0:T(8,128)(2,1)} %get-tuple-element.87), channel_id=1, source_target_pairs={{0,4},{1,5},{2,6},{3,7},{4,0},{5,1},{6,2},{7,3},{8,12},{9,13},{10,... | collective-permute-start | bytes 7077896 | tf_op jit(solution)/shard_map/ppermute | solution.py:595
  308.0 5.8 %copy-start.17 = (f32[1,768]{1,0:T(1,128)S(1)}, f32[1,768]{1,0:T(1,128)}, u32[]{:S(2)}) copy-start(f32[1,768]{1,0:T(1,128)} %get-tuple-element.93) | copy-start | bytes 9220
  308.0 5.9 %copy-start.16 = (f32[1,768]{1,0:T(1,128)S(1)}, f32[1,768]{1,0:T(1,128)}, u32[]{:S(2)}) copy-start(f32[1,768]{1,0:T(1,128)} %get-tuple-element.94) | copy-start | bytes 9220
  310.0 30.2 %collective-permute-start.11 = (bf16[2,4,192,768]{3,2,1,0:T(8,128)(2,1)}, bf16[2,4,192,768]{3,2,1,0:T(8,128)(2,1)}, u32[]{:S(2)}, u32[]{:S(2)}) collective-permute-start(bf16[2,4,192,768]{3,2,1,0:T(8,128)(2,1)} %fusion.2), channel_id=1, source_target_pairs={{0,8},{1,9},{2,10},{3,11},{4,20},{5,21},{6,22},{7,23},{8,0},{9,1},... | collective-permute-start | bytes 7077896 | tf_op jit(solution)/shard_map/ppermute | solution.py:595
  316.6 97.3 %all-gather.7.cloned.1.call-start = ((), (), s32[]{:S(2)}) async-start(), calls=%async_computation.5 | async-start | bytes 2875392 | tf_op jit(solution)/shard_map/all_gather | solution.py:809
  344.3 18.8 %collective-permute-start.12 = (bf16[2,4,96,768]{3,2,1,0:T(8,128)(2,1)S(1)}, bf16[2,4,96,768]{3,2,1,0:T(8,128)(2,1)S(1)}, u32[]{:S(2)}, u32[]{:S(2)}) collective-permute-start(bf16[2,4,96,768]{3,2,1,0:T(8,128)(2,1)S(1)} %constant_dynamic-slice_fusion), channel_id=1, source_target_pairs={{0,16},{1,17},{2,18},{3,19},{4,12},{5,13},{6,14},{7,15},{8,24},{9,... | collective-permute-start | bytes 3538952 | tf_op jit(solution)/shard_map/ppermute | solution.py:595
  364.7 7.0 %collective-permute-start.13 = (bf16[2,96,768]{2,1,0:T(8,128)(2,1)S(1)}, bf16[2,96,768]{2,1,0:T(8,128)(2,1)S(1)}, u32[]{:S(2)}, u32[]{:S(2)}) collective-permute-start(bf16[2,96,768]{2,1,0:T(8,128)(2,1)S(1)} %get-tuple-element.111), channel_id=1, source_target_pairs={{0,1},{1,2},{2,3},{3,0},{4,5},{5,6},{6,7},{7,4},{8,9},{9,10},{10,1... | collective-permute-start | bytes 884744 | tf_op jit(solution)/shard_map/ppermute | solution.py:595
  364.8 23.9 %collective-permute-start.14 = (bf16[2,96,768]{2,1,0:T(8,128)(2,1)S(1)}, bf16[2,96,768]{2,1,0:T(8,128)(2,1)S(1)}, u32[]{:S(2)}, u32[]{:S(2)}) collective-permute-start(bf16[2,96,768]{2,1,0:T(8,128)(2,1)S(1)} %get-tuple-element.113), channel_id=1, source_target_pairs={{0,2},{1,3},{2,0},{3,1},{4,6},{5,7},{6,4},{7,5},{8,10},{9,11},{10,... | collective-permute-start | bytes 884744 | tf_op jit(solution)/shard_map/ppermute | solution.py:595
  364.9 23.8 %collective-permute-start.15 = (bf16[2,96,768]{2,1,0:T(8,128)(2,1)S(1)}, bf16[2,96,768]{2,1,0:T(8,128)(2,1)S(1)}, u32[]{:S(2)}, u32[]{:S(2)}) collective-permute-start(bf16[2,96,768]{2,1,0:T(8,128)(2,1)S(1)} %get-tuple-element.112), channel_id=1, source_target_pairs={{0,3},{1,0},{2,1},{3,2},{4,7},{5,4},{6,5},{7,6},{8,11},{9,8},{10,9... | collective-permute-start | bytes 884744 | tf_op jit(solution)/shard_map/ppermute | solution.py:595
  388.8 5.9 %collective-permute-start.16 = (bf16[2,96,768]{2,1,0:T(8,128)(2,1)S(1)}, bf16[2,96,768]{2,1,0:T(8,128)(2,1)S(1)}, u32[]{:S(2)}, u32[]{:S(2)}) collective-permute-start(bf16[2,96,768]{2,1,0:T(8,128)(2,1)S(1)} %fusion.6), channel_id=1, source_target_pairs={{0,16},{1,17},{2,18},{3,19},{4,12},{5,13},{6,14},{7,15},{8,24},{9,... | collective-permute-start | bytes 884744 | tf_op jit(solution)/shard_map/ppermute | solution.py:595
  395.0 9.1 %collective-permute-start.17 = (bf16[2,192,768]{2,1,0:T(8,128)(2,1)S(1)}, bf16[2,192,768]{2,1,0:T(8,128)(2,1)S(1)}, u32[]{:S(2)}, u32[]{:S(2)}) collective-permute-start(bf16[2,192,768]{2,1,0:T(8,128)(2,1)S(1)} %maximum_select_fusion.5), channel_id=1, source_target_pairs={{0,8},{1,9},{2,10},{3,11},{4,20},{5,21},{6,22},{7,23},{8,0},{9,1},... | collective-permute-start | bytes 1769480 | tf_op jit(solution)/shard_map/ppermute | solution.py:595
  404.5 6.6 %collective-permute-start.18 = (bf16[2,384,768]{2,1,0:T(8,128)(2,1)S(1)}, bf16[2,384,768]{2,1,0:T(8,128)(2,1)S(1)}, u32[]{:S(2)}, u32[]{:S(2)}) collective-permute-start(bf16[2,384,768]{2,1,0:T(8,128)(2,1)S(1)} %maximum_select_fusion.4), channel_id=1, source_target_pairs={{0,4},{1,5},{2,6},{3,7},{4,0},{5,1},{6,2},{7,3},{8,12},{9,13},{10,... | collective-permute-start | bytes 3538952 | tf_op jit(solution)/shard_map/ppermute | solution.py:595
  (10 other events, 27.8 us)
Sparse Core Ops, SparseCore 0:
  26.3 104.4 all-gather.4
  205.3 76.0 reduce-scatter.2
  316.7 26.7 reduce-scatter.4
  345.5 31.6 all-gather.6
